TPU v7x, 256 devices: a whole 4x4x8 slice. The times are simulated.
256 devices in a mesh: row: 4 (over y), col: 16 (over x, z_lo, core), depth: 4 (over z_hi).
Axes of the slice: x: 4, y: 4, z: 8 (z_hi: 4, z_lo: 2; z = z_hi * 2 + z_lo), core: 2. Of those that a mesh axis runs over, the one named last changes fastest.
Arguments:
- coverage: bfloat16 [12288, 16384], P('row', 'col'), may hold values from 0 to 8
- block_mask: int32 [96, 128], P('row', 'col'), may hold values from 0 to 1
- edge_prior: bfloat16 [16384, 512], P('col', 'depth'), may hold values from 0.25 to 4
- test_cost: int32 [12288, 512], P('row', 'depth'), may hold values from 1 to 16
Outputs:
- edge_weights: float32 [16384, 512], P('col', 'depth')
- primal: float32 [12288, 512], P(('row', 'col'), 'depth')
All inputs are finite; a program needn't handle non-finite values.
Results may differ from a plain program's by a relative error of at most 0.0003.
Values may be sent and summed in bfloat16 or wider, within the bound.
No kernel may reach another device: no remote copies, remote signals or barrier semaphores. Data moves between devices by JAX's collectives and lax.ppermute only.
A program may use at most 64 MiB of HBM per device.

v0:
```python
import functools

import jax
import jax.numpy as jnp
from jax import lax
from jax.experimental import pallas as pl
from jax.experimental.pallas import tpu as pltpu
from jax.sharding import PartitionSpec as P

EDGES = 16384
SCEN = 512
BLOCK = 128
ITERS = 2
TESTS = 12288
CHUNK = 192
PAIR = 2 * CHUNK
HALF = 4 * PAIR
WITH_SUMS = PAIR + 8
GATHERED = PAIR + 32
VMEM_LIMIT = 16 * 1024 * 1024
IN_VMEM = pl.BlockSpec(memory_space=pltpu.VMEM)
IN_SMEM = pl.BlockSpec(memory_space=pltpu.SMEM)
ANYWHERE = pl.BlockSpec(memory_space=pl.ANY)
IN_HBM = pl.BlockSpec(memory_space=pltpu.HBM)
f32 = jnp.float32
bf16 = jnp.bfloat16


def call(kernel, out_shape, in_specs, out_specs, flops, scratch=()):
    return pl.pallas_call(
        kernel,
        in_specs=in_specs,
        out_specs=out_specs,
        out_shape=out_shape,
        scratch_shapes=list(scratch),
        compiler_params=pltpu.CompilerParams(vmem_limit_bytes=VMEM_LIMIT),
        cost_estimate=pl.CostEstimate(flops=flops, bytes_accessed=flops // 400, transcendentals=0),
    )


def in_vmem(value):
    return pltpu.with_memory_space_constraint(value, pltpu.VMEM)


def in_hbm(value):
    return pltpu.with_memory_space_constraint(value, pltpu.HBM)


def first_scores_kernel(place_ref, mask_ref, cover_ref, prior_ref, out_ref, kept_ref, weights_ref, tiles_ref, rows_ref, sems):
    def chunk(d, z):
        return lax.rem(place_ref[0] + d, 4) * 4 + z * 2 + place_ref[1]

    tiles = pltpu.make_async_copy(mask_ref, tiles_ref, sems.at[9])
    tiles.start()
    copies = []
    for d in range(4):
        for z in range(2):
            spot = d * 2 + z
            rows = pl.ds(pl.multiple_of(chunk(d, z) * CHUNK, CHUNK), CHUNK)
            copy = pltpu.make_async_copy(
                cover_ref.at[rows, :], kept_ref.at[pl.ds(spot * CHUNK, CHUNK), :], sems.at[spot]
            )
            copy.start()
            copies.append(copy)
    weights = pltpu.make_async_copy(prior_ref, weights_ref, sems.at[8])
    weights.start()
    edges = cover_ref.shape[1]
    tiles.wait()
    column = lax.broadcasted_iota(jnp.int32, (tiles_ref.shape[1], edges), 1) // BLOCK
    spread = column == lax.broadcasted_iota(jnp.int32, column.shape, 0)
    rows_ref[...] = jnp.dot(
        tiles_ref[...].astype(f32), spread.astype(f32), preferred_element_type=f32
    )
    weights.wait()
    ones = jnp.ones((8, edges), bf16)
    half = BLOCK // 2
    for d in range(4):
        for z in range(2):
            spot = d * 2 + z
            copies[spot].wait()
            for j in range(CHUNK // half):
                block_row = (chunk(d, z) * (CHUNK // half) + j) // 2
                entry = jnp.broadcast_to(rows_ref[pl.ds(block_row, 1), :], (16, edges)).astype(bf16)
                for k in range(half // 16):
                    at = spot * CHUNK + j * half + k * 16
                    kept_ref[at : at + 16, :] = kept_ref[at : at + 16, :] * entry
        kept = kept_ref[d * PAIR : (d + 1) * PAIR, :]
        at = d * WITH_SUMS
        out_ref[at : at + PAIR, :] = jnp.dot(kept, weights_ref[...], preferred_element_type=f32)
        sums = lax.dot_general(ones, kept, (((1,), (1,)), ((), ())), preferred_element_type=f32)
        out_ref[at + PAIR : at + WITH_SUMS, :] = jnp.concatenate(
            [sums[:1, j * BLOCK : (j + 1) * BLOCK] for j in range(3)] + [jnp.zeros((5, BLOCK), f32)], axis=0
        )


def first_scores(cover, mask, prior, place):
    edges, scen = prior.shape
    return call(
        first_scores_kernel,
        [jax.ShapeDtypeStruct((4 * WITH_SUMS, scen), f32), pltpu.VMEM((HALF, edges), bf16)],
        [IN_SMEM, IN_HBM, IN_HBM, IN_HBM],
        [IN_VMEM, IN_VMEM],
        2 * HALF * edges * scen,
        [
            pltpu.VMEM(prior.shape, prior.dtype),
            pltpu.VMEM(mask.shape, mask.dtype),
            pltpu.VMEM((mask.shape[0], edges), f32),
            pltpu.SemaphoreType.DMA((10,)),
        ],
    )(place, in_hbm(mask), in_hbm(cover), in_hbm(prior))


def scores_kernel(kept_ref, weights_ref, out_ref):
    for d in range(4):
        rows = slice(d * PAIR, (d + 1) * PAIR)
        out_ref[rows, :] = jnp.dot(kept_ref[rows, :], weights_ref[...], preferred_element_type=f32)


def later_scores(kept, weights):
    edges, scen = weights.shape
    return call(
        scores_kernel,
        jax.ShapeDtypeStruct((HALF, scen), f32),
        [IN_VMEM, IN_VMEM],
        IN_VMEM,
        2 * HALF * edges * scen,
    )(in_vmem(kept), weights)


def flip_kernel(own_ref, other_ref, after_ref, own_out, other_out):
    for kept_ref, out_ref in ((own_ref, own_out), (other_ref, other_out)):
        for d in range(4):
            tile = kept_ref[pl.ds((4 - d) % 4 * PAIR, PAIR), :]
            out_ref[:, d * PAIR : (d + 1) * PAIR] = tile.T


def flip(own, other, after):
    edges = own.shape[1]
    return call(
        flip_kernel,
        [pltpu.VMEM((edges, HALF), bf16), pltpu.VMEM((edges, HALF), bf16)],
        [IN_VMEM, IN_VMEM, ANYWHERE],
        [IN_VMEM, IN_VMEM],
        16 * HALF * edges * 128,
    )(in_vmem(own), in_vmem(other), after)


def column_sums(low):
    return jnp.dot(jnp.ones((8, low.shape[0]), bf16), low, preferred_element_type=f32)


def add_loads(flipped_ref, low_ref, load, size):
    stride = low_ref.shape[0] // 4
    for d in range(4):
        low = low_ref[d * stride : d * stride + PAIR, :]
        load += jnp.dot(flipped_ref[:, d * PAIR : (d + 1) * PAIR], low, preferred_element_type=f32)
        size += column_sums(low)
    return load, size


def half_loads_kernel(flipped_ref, low_ref, load_ref, size_ref):
    load, size = add_loads(flipped_ref, low_ref, jnp.zeros(load_ref.shape, f32), jnp.zeros(size_ref.shape, f32))
    load_ref[...] = load
    size_ref[...] = size


def whole_loads_kernel(flipped_ref, low_ref, load_in, size_in, load_ref, power_ref):
    load, size = add_loads(flipped_ref, low_ref, load_in[...], size_in[...])
    power = jnp.floor(jnp.log2(jnp.maximum(size, 1e-30)))
    load_ref[...] = load * jnp.exp2(11.0 - power[:1, :])
    power_ref[...] = power


def loads(kernel, flipped, low, *so_far):
    edges, scen = flipped.shape[0], low.shape[1]
    return call(
        kernel,
        [jax.ShapeDtypeStruct((edges, scen), f32), jax.ShapeDtypeStruct((8, scen), f32)],
        [IN_VMEM] * (2 + len(so_far)),
        [IN_VMEM, IN_VMEM],
        2 * HALF * edges * scen,
    )(in_vmem(flipped), low, *so_far)


def total_kernel(sums_own, sums_away, low_own, low_away, out_ref):
    totals = [jnp.zeros((32, BLOCK), f32) for _ in range(3)]
    stride = low_own.shape[0] // 4
    for sums_ref, low_ref in ((sums_own, low_own), (sums_away, low_away)):
        for d in range(4):
            sums = sums_ref[d * GATHERED + PAIR : (d + 1) * GATHERED, :]
            for j in range(3):
                low = low_ref[d * stride + j * BLOCK : d * stride + (j + 1) * BLOCK, :]
                totals[j] += jnp.dot(sums, low, preferred_element_type=f32)
    row = lax.broadcasted_iota(jnp.int32, (32, BLOCK), 0)
    total = jnp.zeros((32, BLOCK), f32)
    for j in range(3):
        total += jnp.where(row % 8 == j, totals[j], 0.0)
    out_ref[...] = jnp.full(out_ref.shape, jnp.sum(total), f32)


def total_load(sums_own, sums_away, low_own, low_away):
    return call(
        total_kernel,
        jax.ShapeDtypeStruct((8, low_own.shape[1]), f32),
        [IN_VMEM] * 4,
        IN_VMEM,
        10**8,
    )(sums_own, sums_away, low_own, low_away)


def bf16_parts(sums):
    parts = []
    left = sums
    for _ in range(3):
        part = lax.reduce_precision(left, 8, 7)
        left = left - part
        parts.append(part)
    return parts + [jnp.zeros_like(sums)]


def pack_sums(value):
    return jnp.concatenate([value[:PAIR]] + bf16_parts(value[PAIR:]), axis=0).astype(bf16)


def unpack_sums(value):
    value = value.astype(f32)
    sums = value[PAIR : PAIR + 8] + value[PAIR + 8 : PAIR + 16] + value[PAIR + 16 : PAIR + 24]
    return jnp.concatenate([value[:PAIR], sums], axis=0)


def pack_int16(value):
    top = jnp.max(value, axis=0, keepdims=True)
    power = jnp.ceil(jnp.log2(jnp.maximum(top, 1e-30)))
    code = jnp.round(value * jnp.exp2(16.0 - power)) - 32768.0
    code = jnp.clip(code, -32768.0, 32767.0)
    tile = jnp.broadcast_to(power, (16, value.shape[1]))
    return jnp.concatenate([code, tile], axis=0).astype(jnp.int32).astype(jnp.int16)


def unpack_int16(value):
    value = value.astype(jnp.int32).astype(f32)
    return (value[:-16] + 32768.0) * jnp.exp2(value[-16:-15] - 16.0)


def pack_load(load, power, total):
    scale = jnp.floor(jnp.log2(jnp.maximum(total, 1e-30)))
    total = total * jnp.exp2(-scale)
    high = lax.reduce_precision(total, 5, 10)
    wire = jnp.concatenate([load, power, scale, high, (total - high) * 1024.0], axis=0)
    return lax.reduce_precision(wire, 5, 10)


def unpack_load(wire):
    wire = wire.astype(f32)
    power, scale, high, low = (wire[at : at + 1] for at in range(wire.shape[0] - 32, wire.shape[0], 8))
    return wire[:-32] * jnp.exp2(power - 11.0), (high + low * (1.0 / 1024.0)) * jnp.exp2(scale)


def ring(n, d, stride=1):
    return [(i, (i + d * stride) % n) for i in range(n)]


def swap(bit):
    return [(i, i ^ bit) for i in range(16)]


def shifts(value, axis):
    return [lax.ppermute(value, axis, ring(4, d)) for d in (1, 2, 3)]


def sum_four(parts):
    zero, one, two, three = parts
    return (zero + two) + (one + three)


def body(coverage, block_mask, edge_prior, test_cost):
    at = lax.axis_index("col")
    x, z, core = at // 4, (at // 2) % 2, at % 2
    place = jnp.stack([x, core]).astype(jnp.int32)
    other = jnp.stack([x, 1 - core]).astype(jnp.int32)
    costs = test_cost.reshape(4, 2, 2, CHUNK, test_cost.shape[1])
    cost = lax.dynamic_slice(costs, (x, 0, core, 0, 0), (1, 2, 1, CHUNK, costs.shape[-1]))
    cost = cost.reshape(PAIR, costs.shape[-1]).astype(f32)

    current = edge_prior.astype(f32)
    low_weights = edge_prior
    for iteration in range(ITERS):
        first = iteration == 0
        pack, unpack = (pack_sums, unpack_sums) if first else (pack_int16, unpack_int16)
        with jax.named_scope("scores"):
            if first:
                away, kept_away = first_scores(coverage, block_mask, edge_prior, other)
                here, kept_here = first_scores(coverage, block_mask, edge_prior, place)
            else:
                away = later_scores(kept_away, low_weights)
                here = later_scores(kept_here, low_weights)
            here = here + lax.ppermute(away, "col", swap(1))
            here = here.reshape(4, -1, here.shape[-1])
        with jax.named_scope("sum_x"):
            parts = [unpack(lax.ppermute(pack(here[d]), "col", ring(16, d, 4))) for d in (1, 2, 3)]
            scores = sum_four([here[0]] + parts)
        if first:
            with jax.named_scope("flip"):
                flipped_here, flipped_away = flip(kept_here, kept_away, scores)
        with jax.named_scope("sum_z"):
            scores = scores + unpack(lax.ppermute(pack(scores), "col", swap(2)))
            ratios = scores[:PAIR] / cost
            low_ratios = ratios.astype(bf16)
            if first:
                sums = [part.astype(bf16) for part in bf16_parts(scores[PAIR:])]
                low_ratios = jnp.concatenate([low_ratios] + sums, axis=0)
        with jax.named_scope("gather"):
            lows = [low_ratios] + [lax.ppermute(low_ratios, "col", ring(16, d, 4)) for d in (1, 2, 3)]
            low_here = jnp.concatenate(lows, axis=0)
            low_away = lax.ppermute(low_here, "col", swap(1))
            if first:
                sums_here, sums_away = low_here, low_away
        with jax.named_scope("total"):
            total = total_load(sums_here, sums_away, low_here, low_away)
            total = sum_four([total] + shifts(total, "depth"))
        with jax.named_scope("loads"):
            half, size = loads(half_loads_kernel, flipped_here, low_here)
            load, power = loads(whole_loads_kernel, flipped_away, low_away, half, size)
        with jax.named_scope("sum_y"):
            wire = pack_load(load, power, total)
            pairs = [unpack_load(part) for part in [wire] + shifts(wire.astype(jnp.float16), "row")]
            edge_load = sum_four([pair[0] for pair in pairs])
            load_mean = sum_four([pair[1] for pair in pairs]) / (EDGES * SCEN) + 1e-06
        with jax.named_scope("update"):
            current = current * jnp.exp(-0.25 * edge_load / load_mean)
            low_weights = current.astype(bf16)
    own = lax.dynamic_slice_in_dim(ratios, z * CHUNK, CHUNK, 0)
    primal = TESTS * own / load_mean
    return (current, primal)


def solution(mesh):
    placed = (P("row", "col"), P("row", "col"), P("col", "depth"), P("row", "depth"))
    return jax.shard_map(
        body,
        mesh=mesh,
        in_specs=placed,
        out_specs=(P("col", "depth"), P(("row", "col"), "depth")),
        check_vma=False,
    )
```

profile of v0, /device:TPU:8, one launch (start us, length us, event | category | flops | bytes accessed | tf_op | source)
XLA Modules:
  0.0 130.5 jit_solution(16121216071031804005)
XLA Ops:
  0.7 1.4 %copy.6.mask_ref = s32[24,8]{1,0:T(8,128)} copy(s32[24,8]{0,1:T(8,128)} %param.5) | data formatting | bytes 1536 | tf_op args[1]
  2.1 5.8 %scores.5 = (f32[1568,128]{1,0:T(8,128)}, bf16[1536,1024]{1,0:T(8,128)(2,1)S(1)}) custom-call(s32[2]{0:T(128)S(1)} %get-tuple-element.91.place_ref, s32[24,8]{1,0:T(8,128)} %copy.6.mask_ref, bf16[3072,1024]{1,0:T(8,128)(2,1)} %cover_ref.3, bf16[1024,128]{1,0:T(8,128)(2,1)} %prior_ref.3), custom_call_target="tpu_custom_call" | custom-call | flops 402653184 | bytes 1006632 | tf_op jit(solution)/shard_map/scores/pallas_call | solution.py:98
  8.0 4.9 %scores.4 = (f32[1568,128]{1,0:T(8,128)S(1)}, bf16[1536,1024]{1,0:T(8,128)(2,1)S(1)}) custom-call(s32[2]{0:T(128)S(1)} %get-tuple-element.90.place_ref, s32[24,8]{1,0:T(8,128)} %copy.6.mask_ref, bf16[3072,1024]{1,0:T(8,128)(2,1)} %cover_ref.3, bf16[1024,128]{1,0:T(8,128)(2,1)} %prior_ref.3), custom_call_target="tpu_custom_call" | custom-call | flops 402653184 | bytes 1006632 | tf_op jit(solution)/shard_map/scores/pallas_call | solution.py:98
  13.0 1.2 fusion.112
  14.3 3.1 %collective-permute-start.1 = (bf16[416,128]{1,0:T(8,128)(2,1)S(1)}, bf16[416,128]{1,0:T(8,128)(2,1)S(1)}, u32[]{:S(2)}, u32[]{:S(2)}) collective-permute-start(bf16[416,128]{1,0:T(8,128)(2,1)S(1)} %constant_dynamic-update-slice_fusion), channel_id=1, source_target_pairs={{0,32},{4,36},{8,40},{12,44},{16,48},{20,52},{24,56},{28,60},{32,0... | collective-permute-start | bytes 319496 | tf_op jit(solution)/shard_map/sum_x/ppermute | solution.py:300
  17.5 1.1 collective-permute-start.3
  19.5 4.2 %collective-permute-done.3 = bf16[416,128]{1,0:T(8,128)(2,1)S(1)} collective-permute-done((bf16[416,128]{1,0:T(8,128)(2,1)S(1)}, bf16[416,128]{1,0:T(8,128)(2,1)S(1)}, u32[]{:S(2)}, u32[]{:S(2)}) %collective-permute-start.3) | collective-permute-done | bytes 106528 | tf_op jit(solution)/shard_map/sum_x/ppermute | solution.py:300
  24.9 2.0 %collective-permute-start.4 = (bf16[416,128]{1,0:T(8,128)(2,1)S(1)}, bf16[416,128]{1,0:T(8,128)(2,1)S(1)}, u32[]{:S(2)}, u32[]{:S(2)}) collective-permute-start(bf16[416,128]{1,0:T(8,128)(2,1)S(1)} %constant_dynamic-update-slice_fusion.12), channel_id=1, source_target_pairs={{0,8},{4,12},{8,0},{12,4},{16,24},{20,28},{24,16},{28,20},{32,40},... | collective-permute-start | bytes 319496 | tf_op jit(solution)/shard_map/sum_z/ppermute | solution.py:306
  27.8 1.8 %collective-permute-done.4 = bf16[416,128]{1,0:T(8,128)(2,1)S(1)} collective-permute-done((bf16[416,128]{1,0:T(8,128)(2,1)S(1)}, bf16[416,128]{1,0:T(8,128)(2,1)S(1)}, u32[]{:S(2)}, u32[]{:S(2)}) %collective-permute-start.4) | collective-permute-done | bytes 106528 | tf_op jit(solution)/shard_map/sum_z/ppermute | solution.py:306
  29.9 2.2 %collective-permute-start.7 = (bf16[416,128]{1,0:T(8,128)(2,1)S(1)}, bf16[416,128]{1,0:T(8,128)(2,1)S(1)}, u32[]{:S(2)}, u32[]{:S(2)}) collective-permute-start(bf16[416,128]{1,0:T(8,128)(2,1)S(1)} %constant_dynamic-update-slice_fusion.16), channel_id=1, source_target_pairs={{0,48},{4,52},{8,56},{12,60},{16,0},{20,4},{24,8},{28,12},{32,16},... | collective-permute-start | bytes 319496 | tf_op jit(solution)/shard_map/gather/ppermute | solution.py:313
  33.7 6.2 %collective-permute-done.5 = bf16[416,128]{1,0:T(8,128)(2,1)S(1)} collective-permute-done((bf16[416,128]{1,0:T(8,128)(2,1)S(1)}, bf16[416,128]{1,0:T(8,128)(2,1)S(1)}, u32[]{:S(2)}, u32[]{:S(2)}) %collective-permute-start.5) | collective-permute-done | bytes 106528 | tf_op jit(solution)/shard_map/gather/ppermute | solution.py:313
  40.2 1.7 %flip.1 = (bf16[1024,1536]{1,0:T(8,128)(2,1)S(1)}, bf16[1024,1536]{1,0:T(8,128)(2,1)S(1)}) custom-call(bf16[1536,1024]{1,0:T(8,128)(2,1)S(1)} %get-tuple-element.16.own_ref.kept_ref, bf16[1536,1024]{1,0:T(8,128)(2,1)S(1)} %get-tuple-element.17.other_ref.kept_ref, f32[392,128]{1,0:T(8,128)S(1)} %fusion.18.after_ref), custom_call_target="tpu_custom_call" | custom-call | flops 3221225472 | bytes 8053063 | tf_op jit(solution)/shard_map/flip/pallas_call | solution.py:139
  41.9 1.1 loads.4
  43.5 6.0 %collective-permute-start.11 = (f32[8,128]{1,0:T(8,128)S(1)}, f32[8,128]{1,0:T(8,128)S(1)}, u32[]{:S(2)}, u32[]{:S(2)}) collective-permute-start(f32[8,128]{1,0:T(8,128)S(1)} %total.2), channel_id=1, source_target_pairs={{0,3},{1,0},{2,1},{3,2},{4,7},{5,4},{6,5},{7,6},{8,11},{9,8},{10,9... | collective-permute-start | bytes 12296 | tf_op jit(solution)/shard_map/total/ppermute | solution.py:268
  49.5 3.8 %collective-permute-start.9 = (f32[8,128]{1,0:T(8,128)S(1)}, f32[8,128]{1,0:T(8,128)S(1)}, u32[]{:S(2)}, u32[]{:S(2)}) collective-permute-start(f32[8,128]{1,0:T(8,128)S(1)} %total.2), channel_id=1, source_target_pairs={{0,2},{1,3},{2,0},{3,1},{4,6},{5,7},{6,4},{7,5},{8,10},{9,11},{10,... | collective-permute-start | bytes 12296 | tf_op jit(solution)/shard_map/total/ppermute | solution.py:268
  53.3 1.2 loads.5
  55.2 1.8 %collective-permute-done.9 = f32[8,128]{1,0:T(8,128)S(1)} collective-permute-done((f32[8,128]{1,0:T(8,128)S(1)}, f32[8,128]{1,0:T(8,128)S(1)}, u32[]{:S(2)}, u32[]{:S(2)}) %collective-permute-start.9) | collective-permute-done | bytes 4128 | tf_op jit(solution)/shard_map/total/ppermute | solution.py:268
  57.9 1.6 %collective-permute-start.13 = (f16[1056,128]{1,0:T(8,128)(2,1)S(1)}, f16[1056,128]{1,0:T(8,128)(2,1)S(1)}, u32[]{:S(2)}, u32[]{:S(2)}) collective-permute-start(f16[1056,128]{1,0:T(8,128)(2,1)S(1)} %get-tuple-element.78), channel_id=1, source_target_pairs={{0,64},{64,128},{128,192},{192,0},{1,65},{65,129},{129,193},{193,1... | collective-permute-start | bytes 811016 | tf_op jit(solution)/shard_map/sum_y/ppermute | solution.py:268
  59.5 3.5 %collective-permute-start.12 = (f16[1056,128]{1,0:T(8,128)(2,1)S(1)}, f16[1056,128]{1,0:T(8,128)(2,1)S(1)}, u32[]{:S(2)}, u32[]{:S(2)}) collective-permute-start(f16[1056,128]{1,0:T(8,128)(2,1)S(1)} %get-tuple-element.78), channel_id=1, source_target_pairs={{0,128},{64,192},{128,0},{192,64},{1,129},{65,193},{129,1},{193,65... | collective-permute-start | bytes 811016 | tf_op jit(solution)/shard_map/sum_y/ppermute | solution.py:268
  63.0 2.9 %collective-permute-done.14 = f16[1056,128]{1,0:T(8,128)(2,1)S(1)} collective-permute-done((f16[1056,128]{1,0:T(8,128)(2,1)S(1)}, f16[1056,128]{1,0:T(8,128)(2,1)S(1)}, u32[]{:S(2)}, u32[]{:S(2)}) %collective-permute-start.14) | collective-permute-done | bytes 270368 | tf_op jit(solution)/shard_map/sum_y/ppermute | solution.py:268
  65.9 2.4 %collective-permute-done.13 = f16[1056,128]{1,0:T(8,128)(2,1)S(1)} collective-permute-done((f16[1056,128]{1,0:T(8,128)(2,1)S(1)}, f16[1056,128]{1,0:T(8,128)(2,1)S(1)}, u32[]{:S(2)}, u32[]{:S(2)}) %collective-permute-start.13) | collective-permute-done | bytes 270368 | tf_op jit(solution)/shard_map/sum_y/ppermute | solution.py:268
  68.3 3.4 %collective-permute-done.12 = f16[1056,128]{1,0:T(8,128)(2,1)S(1)} collective-permute-done((f16[1056,128]{1,0:T(8,128)(2,1)S(1)}, f16[1056,128]{1,0:T(8,128)(2,1)S(1)}, u32[]{:S(2)}, u32[]{:S(2)}) %collective-permute-start.12) | collective-permute-done | bytes 270368 | tf_op jit(solution)/shard_map/sum_y/ppermute | solution.py:268
  71.8 1.0 fusion.110
  72.8 1.0 scores.7
  73.9 1.0 scores.6
  74.9 1.3 collective-permute-done.15
  76.7 3.5 %collective-permute-start.18 = (s16[400,128]{1,0:T(8,128)(2,1)S(1)}, s16[400,128]{1,0:T(8,128)(2,1)S(1)}, u32[]{:S(2)}, u32[]{:S(2)}) collective-permute-start(s16[400,128]{1,0:T(8,128)(2,1)S(1)} %fusion.16), channel_id=1, source_target_pairs={{0,48},{4,52},{8,56},{12,60},{16,0},{20,4},{24,8},{28,12},{32,16},... | collective-permute-start | bytes 307208 | tf_op jit(solution)/shard_map/sum_x/ppermute | solution.py:300
  80.3 2.4 %collective-permute-done.17 = s16[400,128]{1,0:T(8,128)(2,1)S(1)} collective-permute-done((s16[400,128]{1,0:T(8,128)(2,1)S(1)}, s16[400,128]{1,0:T(8,128)(2,1)S(1)}, u32[]{:S(2)}, u32[]{:S(2)}) %collective-permute-start.17) | collective-permute-done | bytes 102432 | tf_op jit(solution)/shard_map/sum_x/ppermute | solution.py:300
  82.8 1.7 %collective-permute-done.18 = s16[400,128]{1,0:T(8,128)(2,1)S(1)} collective-permute-done((s16[400,128]{1,0:T(8,128)(2,1)S(1)}, s16[400,128]{1,0:T(8,128)(2,1)S(1)}, u32[]{:S(2)}, u32[]{:S(2)}) %collective-permute-start.18) | collective-permute-done | bytes 102432 | tf_op jit(solution)/shard_map/sum_x/ppermute | solution.py:300
  84.6 1.9 %collective-permute-done.16 = s16[400,128]{1,0:T(8,128)(2,1)S(1)} collective-permute-done((s16[400,128]{1,0:T(8,128)(2,1)S(1)}, s16[400,128]{1,0:T(8,128)(2,1)S(1)}, u32[]{:S(2)}, u32[]{:S(2)}) %collective-permute-start.16) | collective-permute-done | bytes 102432 | tf_op jit(solution)/shard_map/sum_x/ppermute | solution.py:300
  86.7 1.1 collective-permute-start.19
  87.8 3.6 %collective-permute-done.19 = s16[400,128]{1,0:T(8,128)(2,1)S(1)} collective-permute-done((s16[400,128]{1,0:T(8,128)(2,1)S(1)}, s16[400,128]{1,0:T(8,128)(2,1)S(1)}, u32[]{:S(2)}, u32[]{:S(2)}) %collective-permute-start.19) | collective-permute-done | bytes 102432 | tf_op jit(solution)/shard_map/sum_z/ppermute | solution.py:306
  91.6 1.9 %collective-permute-start.22 = (bf16[384,128]{1,0:T(8,128)(2,1)S(1)}, bf16[384,128]{1,0:T(8,128)(2,1)S(1)}, u32[]{:S(2)}, u32[]{:S(2)}) collective-permute-start(bf16[384,128]{1,0:T(8,128)(2,1)S(1)} %get-tuple-element.35), channel_id=1, source_target_pairs={{0,48},{4,52},{8,56},{12,60},{16,0},{20,4},{24,8},{28,12},{32,16},... | collective-permute-start | bytes 294920 | tf_op jit(solution)/shard_map/gather/ppermute | solution.py:313
  93.5 1.0 collective-permute-start.20
  94.4 2.3 %collective-permute-done.22 = bf16[384,128]{1,0:T(8,128)(2,1)S(1)} collective-permute-done((bf16[384,128]{1,0:T(8,128)(2,1)S(1)}, bf16[384,128]{1,0:T(8,128)(2,1)S(1)}, u32[]{:S(2)}, u32[]{:S(2)}) %collective-permute-start.22) | collective-permute-done | bytes 98336 | tf_op jit(solution)/shard_map/gather/ppermute | solution.py:313
  96.7 3.0 %collective-permute-done.21 = bf16[384,128]{1,0:T(8,128)(2,1)S(1)} collective-permute-done((bf16[384,128]{1,0:T(8,128)(2,1)S(1)}, bf16[384,128]{1,0:T(8,128)(2,1)S(1)}, u32[]{:S(2)}, u32[]{:S(2)}) %collective-permute-start.21) | collective-permute-done | bytes 98336 | tf_op jit(solution)/shard_map/gather/ppermute | solution.py:313
  100.5 1.1 loads.6
  102.6 3.9 %collective-permute-start.26 = (f32[8,128]{1,0:T(8,128)S(1)}, f32[8,128]{1,0:T(8,128)S(1)}, u32[]{:S(2)}, u32[]{:S(2)}) collective-permute-start(f32[8,128]{1,0:T(8,128)S(1)} %total.3), channel_id=1, source_target_pairs={{0,3},{1,0},{2,1},{3,2},{4,7},{5,4},{6,5},{7,6},{8,11},{9,8},{10,9... | collective-permute-start | bytes 12296 | tf_op jit(solution)/shard_map/total/ppermute | solution.py:268
  106.6 2.6 %collective-permute-start.24 = (f32[8,128]{1,0:T(8,128)S(1)}, f32[8,128]{1,0:T(8,128)S(1)}, u32[]{:S(2)}, u32[]{:S(2)}) collective-permute-start(f32[8,128]{1,0:T(8,128)S(1)} %total.3), channel_id=1, source_target_pairs={{0,2},{1,3},{2,0},{3,1},{4,6},{5,7},{6,4},{7,5},{8,10},{9,11},{10,... | collective-permute-start | bytes 12296 | tf_op jit(solution)/shard_map/total/ppermute | solution.py:268
  109.2 1.2 loads.7
  110.4 1.9 %collective-permute-done.25 = f32[8,128]{1,0:T(8,128)S(1)} collective-permute-done((f32[8,128]{1,0:T(8,128)S(1)}, f32[8,128]{1,0:T(8,128)S(1)}, u32[]{:S(2)}, u32[]{:S(2)}) %collective-permute-start.25) | collective-permute-done | bytes 4128 | tf_op jit(solution)/shard_map/total/ppermute | solution.py:268
  112.3 1.8 %collective-permute-done.24 = f32[8,128]{1,0:T(8,128)S(1)} collective-permute-done((f32[8,128]{1,0:T(8,128)S(1)}, f32[8,128]{1,0:T(8,128)S(1)}, u32[]{:S(2)}, u32[]{:S(2)}) %collective-permute-start.24) | collective-permute-done | bytes 4128 | tf_op jit(solution)/shard_map/total/ppermute | solution.py:268
  114.4 3.5 %collective-permute-start.29 = (f16[1056,128]{1,0:T(8,128)(2,1)S(1)}, f16[1056,128]{1,0:T(8,128)(2,1)S(1)}, u32[]{:S(2)}, u32[]{:S(2)}) collective-permute-start(f16[1056,128]{1,0:T(8,128)(2,1)S(1)} %get-tuple-element.71), channel_id=1, source_target_pairs={{0,192},{64,0},{128,64},{192,128},{1,193},{65,1},{129,65},{193,129... | collective-permute-start | bytes 811016 | tf_op jit(solution)/shard_map/sum_y/ppermute | solution.py:268
  118.0 2.4 %collective-permute-start.27 = (f16[1056,128]{1,0:T(8,128)(2,1)S(1)}, f16[1056,128]{1,0:T(8,128)(2,1)S(1)}, u32[]{:S(2)}, u32[]{:S(2)}) collective-permute-start(f16[1056,128]{1,0:T(8,128)(2,1)S(1)} %get-tuple-element.71), channel_id=1, source_target_pairs={{0,128},{64,192},{128,0},{192,64},{1,129},{65,193},{129,1},{193,65... | collective-permute-start | bytes 811016 | tf_op jit(solution)/shard_map/sum_y/ppermute | solution.py:268
  120.4 4.5 %collective-permute-done.29 = f16[1056,128]{1,0:T(8,128)(2,1)S(1)} collective-permute-done((f16[1056,128]{1,0:T(8,128)(2,1)S(1)}, f16[1056,128]{1,0:T(8,128)(2,1)S(1)}, u32[]{:S(2)}, u32[]{:S(2)}) %collective-permute-start.29) | collective-permute-done | bytes 270368 | tf_op jit(solution)/shard_map/sum_y/ppermute | solution.py:268
  124.9 2.4 %collective-permute-done.28 = f16[1056,128]{1,0:T(8,128)(2,1)S(1)} collective-permute-done((f16[1056,128]{1,0:T(8,128)(2,1)S(1)}, f16[1056,128]{1,0:T(8,128)(2,1)S(1)}, u32[]{:S(2)}, u32[]{:S(2)}) %collective-permute-start.28) | collective-permute-done | bytes 270368 | tf_op jit(solution)/shard_map/sum_y/ppermute | solution.py:268
  127.4 1.3 %collective-permute-done.27 = f16[1056,128]{1,0:T(8,128)(2,1)S(1)} collective-permute-done((f16[1056,128]{1,0:T(8,128)(2,1)S(1)}, f16[1056,128]{1,0:T(8,128)(2,1)S(1)}, u32[]{:S(2)}, u32[]{:S(2)}) %collective-permute-start.27) | collective-permute-done | bytes 270368 | tf_op jit(solution)/shard_map/sum_y/ppermute | solution.py:268
  129.5 1.0 fusion.5
  (116 shorter events, 11.5 us)
Async XLA Ops:
  7.9 5.1 %collective-permute-start = (f32[1568,128]{1,0:T(8,128)}, f32[1568,128]{1,0:T(8,128)}, u32[]{:S(2)}, u32[]{:S(2)}) collective-permute-start(f32[1568,128]{1,0:T(8,128)} %get-tuple-element.19), channel_id=1, source_target_pairs={{0,4},{4,0},{8,12},{12,8},{16,20},{20,16},{24,28},{28,24},{32,36},... | collective-permute-start | bytes 2408456 | tf_op jit(solution)/shard_map/scores/ppermute | solution.py:297
  14.3 10.3 %collective-permute-start.1 = (bf16[416,128]{1,0:T(8,128)(2,1)S(1)}, bf16[416,128]{1,0:T(8,128)(2,1)S(1)}, u32[]{:S(2)}, u32[]{:S(2)}) collective-permute-start(bf16[416,128]{1,0:T(8,128)(2,1)S(1)} %constant_dynamic-update-slice_fusion), channel_id=1, source_target_pairs={{0,32},{4,36},{8,40},{12,44},{16,48},{20,52},{24,56},{28,60},{32,0... | collective-permute-start | bytes 319496 | tf_op jit(solution)/shard_map/sum_x/ppermute | solution.py:300
  17.5 6.2 %collective-permute-start.3 = (bf16[416,128]{1,0:T(8,128)(2,1)S(1)}, bf16[416,128]{1,0:T(8,128)(2,1)S(1)}, u32[]{:S(2)}, u32[]{:S(2)}) collective-permute-start(bf16[416,128]{1,0:T(8,128)(2,1)S(1)} %constant_dynamic-update-slice_fusion.8), channel_id=1, source_target_pairs={{0,48},{4,52},{8,56},{12,60},{16,0},{20,4},{24,8},{28,12},{32,16},... | collective-permute-start | bytes 319496 | tf_op jit(solution)/shard_map/sum_x/ppermute | solution.py:300
  18.6 6.0 %collective-permute-start.2 = (bf16[416,128]{1,0:T(8,128)(2,1)S(1)}, bf16[416,128]{1,0:T(8,128)(2,1)S(1)}, u32[]{:S(2)}, u32[]{:S(2)}) collective-permute-start(bf16[416,128]{1,0:T(8,128)(2,1)S(1)} %constant_dynamic-update-slice_fusion.4), channel_id=1, source_target_pairs={{0,16},{4,20},{8,24},{12,28},{16,32},{20,36},{24,40},{28,44},{32,4... | collective-permute-start | bytes 319496 | tf_op jit(solution)/shard_map/sum_x/ppermute | solution.py:300
  24.9 4.8 %collective-permute-start.4 = (bf16[416,128]{1,0:T(8,128)(2,1)S(1)}, bf16[416,128]{1,0:T(8,128)(2,1)S(1)}, u32[]{:S(2)}, u32[]{:S(2)}) collective-permute-start(bf16[416,128]{1,0:T(8,128)(2,1)S(1)} %constant_dynamic-update-slice_fusion.12), channel_id=1, source_target_pairs={{0,8},{4,12},{8,0},{12,4},{16,24},{20,28},{24,16},{28,20},{32,40},... | collective-permute-start | bytes 319496 | tf_op jit(solution)/shard_map/sum_z/ppermute | solution.py:306
  29.9 10.1 %collective-permute-start.7 = (bf16[416,128]{1,0:T(8,128)(2,1)S(1)}, bf16[416,128]{1,0:T(8,128)(2,1)S(1)}, u32[]{:S(2)}, u32[]{:S(2)}) collective-permute-start(bf16[416,128]{1,0:T(8,128)(2,1)S(1)} %constant_dynamic-update-slice_fusion.16), channel_id=1, source_target_pairs={{0,48},{4,52},{8,56},{12,60},{16,0},{20,4},{24,8},{28,12},{32,16},... | collective-permute-start | bytes 319496 | tf_op jit(solution)/shard_map/gather/ppermute | solution.py:313
  32.1 7.8 %collective-permute-start.6 = (bf16[416,128]{1,0:T(8,128)(2,1)S(1)}, bf16[416,128]{1,0:T(8,128)(2,1)S(1)}, u32[]{:S(2)}, u32[]{:S(2)}) collective-permute-start(bf16[416,128]{1,0:T(8,128)(2,1)S(1)} %constant_dynamic-update-slice_fusion.16), channel_id=1, source_target_pairs={{0,32},{4,36},{8,40},{12,44},{16,48},{20,52},{24,56},{28,60},{32,0... | collective-permute-start | bytes 319496 | tf_op jit(solution)/shard_map/gather/ppermute | solution.py:313
  32.9 7.0 %collective-permute-start.5 = (bf16[416,128]{1,0:T(8,128)(2,1)S(1)}, bf16[416,128]{1,0:T(8,128)(2,1)S(1)}, u32[]{:S(2)}, u32[]{:S(2)}) collective-permute-start(bf16[416,128]{1,0:T(8,128)(2,1)S(1)} %constant_dynamic-update-slice_fusion.16), channel_id=1, source_target_pairs={{0,16},{4,20},{8,24},{12,28},{16,32},{20,36},{24,40},{28,44},{32,4... | collective-permute-start | bytes 319496 | tf_op jit(solution)/shard_map/gather/ppermute | solution.py:313
  40.0 3.1 %collective-permute-start.8 = (bf16[1664,128]{1,0:T(8,128)(2,1)S(1)}, bf16[1664,128]{1,0:T(8,128)(2,1)S(1)}, u32[]{:S(2)}, u32[]{:S(2)}) collective-permute-start(bf16[1664,128]{1,0:T(8,128)(2,1)S(1)} %constant_dynamic-update-slice_fusion.21.low_ref.sums_own.low_own), channel_id=1, source_target_pairs={{0,4},{4,0},{8,12},{12,8},{16,20},{20,16},{24,28},{28,24},{32,36},... | collective-permute-start | bytes 1277960 | tf_op jit(solution)/shard_map/gather/ppermute | solution.py:315
  43.5 11.0 %collective-permute-start.11 = (f32[8,128]{1,0:T(8,128)S(1)}, f32[8,128]{1,0:T(8,128)S(1)}, u32[]{:S(2)}, u32[]{:S(2)}) collective-permute-start(f32[8,128]{1,0:T(8,128)S(1)} %total.2), channel_id=1, source_target_pairs={{0,3},{1,0},{2,1},{3,2},{4,7},{5,4},{6,5},{7,6},{8,11},{9,8},{10,9... | collective-permute-start | bytes 12296 | tf_op jit(solution)/shard_map/total/ppermute | solution.py:268
  49.5 5.7 %collective-permute-start.10 = (f32[8,128]{1,0:T(8,128)S(1)}, f32[8,128]{1,0:T(8,128)S(1)}, u32[]{:S(2)}, u32[]{:S(2)}) collective-permute-start(f32[8,128]{1,0:T(8,128)S(1)} %total.2), channel_id=1, source_target_pairs={{0,1},{1,2},{2,3},{3,0},{4,5},{5,6},{6,7},{7,4},{8,9},{9,10},{10,1... | collective-permute-start | bytes 12296 | tf_op jit(solution)/shard_map/total/ppermute | solution.py:268
  49.5 7.5 %collective-permute-start.9 = (f32[8,128]{1,0:T(8,128)S(1)}, f32[8,128]{1,0:T(8,128)S(1)}, u32[]{:S(2)}, u32[]{:S(2)}) collective-permute-start(f32[8,128]{1,0:T(8,128)S(1)} %total.2), channel_id=1, source_target_pairs={{0,2},{1,3},{2,0},{3,1},{4,6},{5,7},{6,4},{7,5},{8,10},{9,11},{10,... | collective-permute-start | bytes 12296 | tf_op jit(solution)/shard_map/total/ppermute | solution.py:268
  54.5 17.3 %copy-start = (bf16[1024,128]{1,0:T(8,128)(2,1)S(1)}, bf16[1024,128]{1,0:T(8,128)(2,1)}, u32[]{:S(2)}) copy-start(bf16[1024,128]{1,0:T(8,128)(2,1)} %prior_ref.3) | copy-start | bytes 786436
  57.4 8.5 %collective-permute-start.14 = (f16[1056,128]{1,0:T(8,128)(2,1)S(1)}, f16[1056,128]{1,0:T(8,128)(2,1)S(1)}, u32[]{:S(2)}, u32[]{:S(2)}) collective-permute-start(f16[1056,128]{1,0:T(8,128)(2,1)S(1)} %get-tuple-element.78), channel_id=1, source_target_pairs={{0,192},{64,0},{128,64},{192,128},{1,193},{65,1},{129,65},{193,129... | collective-permute-start | bytes 811016 | tf_op jit(solution)/shard_map/sum_y/ppermute | solution.py:268
  57.9 10.4 %collective-permute-start.13 = (f16[1056,128]{1,0:T(8,128)(2,1)S(1)}, f16[1056,128]{1,0:T(8,128)(2,1)S(1)}, u32[]{:S(2)}, u32[]{:S(2)}) collective-permute-start(f16[1056,128]{1,0:T(8,128)(2,1)S(1)} %get-tuple-element.78), channel_id=1, source_target_pairs={{0,64},{64,128},{128,192},{192,0},{1,65},{65,129},{129,193},{193,1... | collective-permute-start | bytes 811016 | tf_op jit(solution)/shard_map/sum_y/ppermute | solution.py:268
  59.5 12.2 %collective-permute-start.12 = (f16[1056,128]{1,0:T(8,128)(2,1)S(1)}, f16[1056,128]{1,0:T(8,128)(2,1)S(1)}, u32[]{:S(2)}, u32[]{:S(2)}) collective-permute-start(f16[1056,128]{1,0:T(8,128)(2,1)S(1)} %get-tuple-element.78), channel_id=1, source_target_pairs={{0,128},{64,192},{128,0},{192,64},{1,129},{65,193},{129,1},{193,65... | collective-permute-start | bytes 811016 | tf_op jit(solution)/shard_map/sum_y/ppermute | solution.py:268
  73.8 2.4 %collective-permute-start.15 = (f32[1536,128]{1,0:T(8,128)S(1)}, f32[1536,128]{1,0:T(8,128)S(1)}, u32[]{:S(2)}, u32[]{:S(2)}) collective-permute-start(f32[1536,128]{1,0:T(8,128)S(1)} %scores.7), channel_id=1, source_target_pairs={{0,4},{4,0},{8,12},{12,8},{16,20},{20,16},{24,28},{28,24},{32,36},... | collective-permute-start | bytes 2359304 | tf_op jit(solution)/shard_map/scores/ppermute | solution.py:297
  76.5 6.2 %collective-permute-start.17 = (s16[400,128]{1,0:T(8,128)(2,1)S(1)}, s16[400,128]{1,0:T(8,128)(2,1)S(1)}, u32[]{:S(2)}, u32[]{:S(2)}) collective-permute-start(s16[400,128]{1,0:T(8,128)(2,1)S(1)} %fusion.15), channel_id=1, source_target_pairs={{0,16},{4,20},{8,24},{12,28},{16,32},{20,36},{24,40},{28,44},{32,4... | collective-permute-start | bytes 307208 | tf_op jit(solution)/shard_map/sum_x/ppermute | solution.py:300
  76.7 7.9 %collective-permute-start.18 = (s16[400,128]{1,0:T(8,128)(2,1)S(1)}, s16[400,128]{1,0:T(8,128)(2,1)S(1)}, u32[]{:S(2)}, u32[]{:S(2)}) collective-permute-start(s16[400,128]{1,0:T(8,128)(2,1)S(1)} %fusion.16), channel_id=1, source_target_pairs={{0,48},{4,52},{8,56},{12,60},{16,0},{20,4},{24,8},{28,12},{32,16},... | collective-permute-start | bytes 307208 | tf_op jit(solution)/shard_map/sum_x/ppermute | solution.py:300
  80.2 6.3 %collective-permute-start.16 = (s16[400,128]{1,0:T(8,128)(2,1)S(1)}, s16[400,128]{1,0:T(8,128)(2,1)S(1)}, u32[]{:S(2)}, u32[]{:S(2)}) collective-permute-start(s16[400,128]{1,0:T(8,128)(2,1)S(1)} %fusion.14), channel_id=1, source_target_pairs={{0,32},{4,36},{8,40},{12,44},{16,48},{20,52},{24,56},{28,60},{32,0... | collective-permute-start | bytes 307208 | tf_op jit(solution)/shard_map/sum_x/ppermute | solution.py:300
  86.7 4.7 %collective-permute-start.19 = (s16[400,128]{1,0:T(8,128)(2,1)S(1)}, s16[400,128]{1,0:T(8,128)(2,1)S(1)}, u32[]{:S(2)}, u32[]{:S(2)}) collective-permute-start(s16[400,128]{1,0:T(8,128)(2,1)S(1)} %fusion.17), channel_id=1, source_target_pairs={{0,8},{4,12},{8,0},{12,4},{16,24},{20,28},{24,16},{28,20},{32,40},... | collective-permute-start | bytes 307208 | tf_op jit(solution)/shard_map/sum_z/ppermute | solution.py:306
  91.6 5.1 %collective-permute-start.22 = (bf16[384,128]{1,0:T(8,128)(2,1)S(1)}, bf16[384,128]{1,0:T(8,128)(2,1)S(1)}, u32[]{:S(2)}, u32[]{:S(2)}) collective-permute-start(bf16[384,128]{1,0:T(8,128)(2,1)S(1)} %get-tuple-element.35), channel_id=1, source_target_pairs={{0,48},{4,52},{8,56},{12,60},{16,0},{20,4},{24,8},{28,12},{32,16},... | collective-permute-start | bytes 294920 | tf_op jit(solution)/shard_map/gather/ppermute | solution.py:313
  93.5 6.2 %collective-permute-start.21 = (bf16[384,128]{1,0:T(8,128)(2,1)S(1)}, bf16[384,128]{1,0:T(8,128)(2,1)S(1)}, u32[]{:S(2)}, u32[]{:S(2)}) collective-permute-start(bf16[384,128]{1,0:T(8,128)(2,1)S(1)} %get-tuple-element.35), channel_id=1, source_target_pairs={{0,32},{4,36},{8,40},{12,44},{16,48},{20,52},{24,56},{28,60},{32,0... | collective-permute-start | bytes 294920 | tf_op jit(solution)/shard_map/gather/ppermute | solution.py:313
  93.5 6.9 %collective-permute-start.20 = (bf16[384,128]{1,0:T(8,128)(2,1)S(1)}, bf16[384,128]{1,0:T(8,128)(2,1)S(1)}, u32[]{:S(2)}, u32[]{:S(2)}) collective-permute-start(bf16[384,128]{1,0:T(8,128)(2,1)S(1)} %get-tuple-element.35), channel_id=1, source_target_pairs={{0,16},{4,20},{8,24},{12,28},{16,32},{20,36},{24,40},{28,44},{32,4... | collective-permute-start | bytes 294920 | tf_op jit(solution)/shard_map/gather/ppermute | solution.py:313
  100.4 1.8 %collective-permute-start.23 = (bf16[1536,128]{1,0:T(8,128)(2,1)S(1)}, bf16[1536,128]{1,0:T(8,128)(2,1)S(1)}, u32[]{:S(2)}, u32[]{:S(2)}) collective-permute-start(bf16[1536,128]{1,0:T(8,128)(2,1)S(1)} %pad_maximum_fusion.low_ref.low_own), channel_id=1, source_target_pairs={{0,4},{4,0},{8,12},{12,8},{16,20},{20,16},{24,28},{28,24},{32,36},... | collective-permute-start | bytes 1179656 | tf_op jit(solution)/shard_map/gather/ppermute | solution.py:315
  102.6 7.8 %collective-permute-start.26 = (f32[8,128]{1,0:T(8,128)S(1)}, f32[8,128]{1,0:T(8,128)S(1)}, u32[]{:S(2)}, u32[]{:S(2)}) collective-permute-start(f32[8,128]{1,0:T(8,128)S(1)} %total.3), channel_id=1, source_target_pairs={{0,3},{1,0},{2,1},{3,2},{4,7},{5,4},{6,5},{7,6},{8,11},{9,8},{10,9... | collective-permute-start | bytes 12296 | tf_op jit(solution)/shard_map/total/ppermute | solution.py:268
  106.6 5.7 %collective-permute-start.25 = (f32[8,128]{1,0:T(8,128)S(1)}, f32[8,128]{1,0:T(8,128)S(1)}, u32[]{:S(2)}, u32[]{:S(2)}) collective-permute-start(f32[8,128]{1,0:T(8,128)S(1)} %total.3), channel_id=1, source_target_pairs={{0,1},{1,2},{2,3},{3,0},{4,5},{5,6},{6,7},{7,4},{8,9},{9,10},{10,1... | collective-permute-start | bytes 12296 | tf_op jit(solution)/shard_map/total/ppermute | solution.py:268
  106.6 7.5 %collective-permute-start.24 = (f32[8,128]{1,0:T(8,128)S(1)}, f32[8,128]{1,0:T(8,128)S(1)}, u32[]{:S(2)}, u32[]{:S(2)}) collective-permute-start(f32[8,128]{1,0:T(8,128)S(1)} %total.3), channel_id=1, source_target_pairs={{0,2},{1,3},{2,0},{3,1},{4,6},{5,7},{6,4},{7,5},{8,10},{9,11},{10,... | collective-permute-start | bytes 12296 | tf_op jit(solution)/shard_map/total/ppermute | solution.py:268
  110.4 19.1 %copy-start.1 = (f32[1024,128]{1,0:T(8,128)S(1)}, f32[1024,128]{1,0:T(8,128)}, u32[]{:S(2)}) copy-start(f32[1024,128]{1,0:T(8,128)} %get-tuple-element.48) | copy-start | bytes 1572868
  114.4 10.5 %collective-permute-start.29 = (f16[1056,128]{1,0:T(8,128)(2,1)S(1)}, f16[1056,128]{1,0:T(8,128)(2,1)S(1)}, u32[]{:S(2)}, u32[]{:S(2)}) collective-permute-start(f16[1056,128]{1,0:T(8,128)(2,1)S(1)} %get-tuple-element.71), channel_id=1, source_target_pairs={{0,192},{64,0},{128,64},{192,128},{1,193},{65,1},{129,65},{193,129... | collective-permute-start | bytes 811016 | tf_op jit(solution)/shard_map/sum_y/ppermute | solution.py:268
  118.0 9.4 %collective-permute-start.28 = (f16[1056,128]{1,0:T(8,128)(2,1)S(1)}, f16[1056,128]{1,0:T(8,128)(2,1)S(1)}, u32[]{:S(2)}, u32[]{:S(2)}) collective-permute-start(f16[1056,128]{1,0:T(8,128)(2,1)S(1)} %get-tuple-element.71), channel_id=1, source_target_pairs={{0,64},{64,128},{128,192},{192,0},{1,65},{65,129},{129,193},{193,1... | collective-permute-start | bytes 811016 | tf_op jit(solution)/shard_map/sum_y/ppermute | solution.py:268
  118.0 10.8 %collective-permute-start.27 = (f16[1056,128]{1,0:T(8,128)(2,1)S(1)}, f16[1056,128]{1,0:T(8,128)(2,1)S(1)}, u32[]{:S(2)}, u32[]{:S(2)}) collective-permute-start(f16[1056,128]{1,0:T(8,128)(2,1)S(1)} %get-tuple-element.71), channel_id=1, source_target_pairs={{0,128},{64,192},{128,0},{192,64},{1,129},{65,193},{129,1},{193,65... | collective-permute-start | bytes 811016 | tf_op jit(solution)/shard_map/sum_y/ppermute | solution.py:268
where the time goes:
time: 133 us; the launch traced here: 130 us
  waiting for transfers between devices  53.7 us (40%)
  starting transfers between devices  47.1 us (35%)
  Pallas kernels  19.8 us (15%)
  other arithmetic  7.02 us (5%)
  local copies, waits for them, and re-layouts  1.65 us (1%)
    ppermute x12, starting transfers between devices, shifts(): return [lax.ppermute(value, axis, ring(4, d)) for d in (1, 2, 3)]  27.9 us
    ppermute x12, waiting for transfers between devices, shifts(): return [lax.ppermute(value, axis, ring(4, d)) for d in (1, 2, 3)]  23 us
    ppermute x6, waiting for transfers between devices, body(): lax.ppermute(low_ratios, 'col', ring(16, d, 4))  12.1 us
    ppermute x6, waiting for transfers between devices, body(): lax.ppermute(pack(here[d]), 'col', ring(16, d, 4))  11.1 us
    pallas_call x2, Pallas kernels, first_scores(): call(first_scores_kernel, [jax.ShapeDtypeStruct((4 * WITH_SUMS, scen), f3...  10.8 us
    ppermute x6, starting transfers between devices, body(): lax.ppermute(pack(here[d]), 'col', ring(16, d, 4))  8.82 us
    ppermute x6, starting transfers between devices, body(): lax.ppermute(low_ratios, 'col', ring(16, d, 4))  6.71 us
    ppermute x2, waiting for transfers between devices, body(): scores = scores + unpack(lax.ppermute(pack(scores), 'col', swap(2)))  5.49 us
  transfers between devices with their start and end apart: 30, of which 23 were waited for; matrix products, arithmetic and copies ran while one was open for 1% of the time, Pallas kernels for 9%

commit v1 on v0

--- a/solution.py
+++ b/solution.py
@@ -46,68 +46,93 @@
     return pltpu.with_memory_space_constraint(value, pltpu.HBM)
 
 
-def first_scores_kernel(place_ref, mask_ref, cover_ref, prior_ref, out_ref, kept_ref, weights_ref, tiles_ref, rows_ref, sems):
-    def chunk(d, z):
-        return lax.rem(place_ref[0] + d, 4) * 4 + z * 2 + place_ref[1]
-
-    tiles = pltpu.make_async_copy(mask_ref, tiles_ref, sems.at[9])
-    tiles.start()
-    copies = []
+def half_scores(kept_ref, weights, rows_ref, place_ref, core, out_ref, raw_ref=None, wait=None):
+    edges = kept_ref.shape[1]
+    half = BLOCK // 2
+    ones = jnp.ones((8, edges), bf16)
     for d in range(4):
         for z in range(2):
             spot = d * 2 + z
-            rows = pl.ds(pl.multiple_of(chunk(d, z) * CHUNK, CHUNK), CHUNK)
-            copy = pltpu.make_async_copy(
-                cover_ref.at[rows, :], kept_ref.at[pl.ds(spot * CHUNK, CHUNK), :], sems.at[spot]
-            )
-            copy.start()
-            copies.append(copy)
-    weights = pltpu.make_async_copy(prior_ref, weights_ref, sems.at[8])
-    weights.start()
-    edges = cover_ref.shape[1]
-    tiles.wait()
-    column = lax.broadcasted_iota(jnp.int32, (tiles_ref.shape[1], edges), 1) // BLOCK
-    spread = column == lax.broadcasted_iota(jnp.int32, column.shape, 0)
-    rows_ref[...] = jnp.dot(
-        tiles_ref[...].astype(f32), spread.astype(f32), preferred_element_type=f32
-    )
-    weights.wait()
-    ones = jnp.ones((8, edges), bf16)
-    half = BLOCK // 2
-    for d in range(4):
-        for z in range(2):
-            spot = d * 2 + z
-            copies[spot].wait()
+            if wait is not None:
+                wait(spot)
+            chunk = lax.rem(place_ref[0] + d, 4) * 4 + z * 2 + core
             for j in range(CHUNK // half):
-                block_row = (chunk(d, z) * (CHUNK // half) + j) // 2
+                block_row = (chunk * (CHUNK // half) + j) // 2
                 entry = jnp.broadcast_to(rows_ref[pl.ds(block_row, 1), :], (16, edges)).astype(bf16)
                 for k in range(half // 16):
                     at = spot * CHUNK + j * half + k * 16
-                    kept_ref[at : at + 16, :] = kept_ref[at : at + 16, :] * entry
+                    source = kept_ref if raw_ref is None else raw_ref
+                    kept_ref[at : at + 16, :] = source[at : at + 16, :] * entry
         kept = kept_ref[d * PAIR : (d + 1) * PAIR, :]
         at = d * WITH_SUMS
-        out_ref[at : at + PAIR, :] = jnp.dot(kept, weights_ref[...], preferred_element_type=f32)
+        out_ref[at : at + PAIR, :] = jnp.dot(kept, weights, preferred_element_type=f32)
         sums = lax.dot_general(ones, kept, (((1,), (1,)), ((), ())), preferred_element_type=f32)
         out_ref[at + PAIR : at + WITH_SUMS, :] = jnp.concatenate(
             [sums[:1, j * BLOCK : (j + 1) * BLOCK] for j in range(3)] + [jnp.zeros((5, BLOCK), f32)], axis=0
         )
 
 
+def first_scores_kernel(place_ref, mask_ref, cover_ref, prior_ref, out_ref, kept_ref, raw_ref, weights_ref, rows_ref, tiles_ref, sems):
+    tiles = pltpu.make_async_copy(mask_ref, tiles_ref, sems.at[16])
+    tiles.start()
+    copies = []
+    for half, held_ref in enumerate((kept_ref, raw_ref)):
+        core = place_ref[1] if half else 1 - place_ref[1]
+        for spot in range(8):
+            chunk = lax.rem(place_ref[0] + spot // 2, 4) * 4 + spot % 2 * 2 + core
+            rows = pl.ds(pl.multiple_of(chunk * CHUNK, CHUNK), CHUNK)
+            copy = pltpu.make_async_copy(
+                cover_ref.at[rows, :], held_ref.at[pl.ds(spot * CHUNK, CHUNK), :], sems.at[half * 8 + spot]
+            )
+            copy.start()
+            copies.append(copy)
+        if half == 0:
+            weights = pltpu.make_async_copy(prior_ref, weights_ref, sems.at[17])
+            weights.start()
+    edges = cover_ref.shape[1]
+    tiles.wait()
+    column = lax.broadcasted_iota(jnp.int32, (tiles_ref.shape[0], edges), 1) // BLOCK
+    spread = column == lax.broadcasted_iota(jnp.int32, column.shape, 0)
+    rows_ref[...] = lax.dot_general(
+        tiles_ref[...].astype(f32), spread.astype(f32), (((0,), (0,)), ((), ())), preferred_element_type=f32
+    )
+    weights.wait()
+    half_scores(
+        kept_ref, weights_ref[...], rows_ref, place_ref, 1 - place_ref[1], out_ref, wait=lambda spot: copies[spot].wait()
+    )
+    for copy in copies[8:]:
+        copy.wait()
+
+
+def own_scores_kernel(place_ref, raw_ref, weights_ref, rows_ref, out_ref, kept_ref):
+    half_scores(kept_ref, weights_ref[...], rows_ref, place_ref, place_ref[1], out_ref, raw_ref=raw_ref)
+
+
 def first_scores(cover, mask, prior, place):
     edges, scen = prior.shape
-    return call(
+    tests = BLOCK * mask.shape[0]
+    away, kept_away, raw, weights, rows = call(
         first_scores_kernel,
-        [jax.ShapeDtypeStruct((4 * WITH_SUMS, scen), f32), pltpu.VMEM((HALF, edges), bf16)],
+        [
+            pltpu.VMEM((4 * WITH_SUMS, scen), f32),
+            pltpu.VMEM((HALF, edges), bf16),
+            pltpu.VMEM((HALF, edges), bf16),
+            pltpu.VMEM(prior.shape, bf16),
+            pltpu.VMEM((tests // BLOCK, edges), f32),
+        ],
         [IN_SMEM, IN_HBM, IN_HBM, IN_HBM],
-        [IN_VMEM, IN_VMEM],
+        [IN_VMEM] * 5,
         2 * HALF * edges * scen,
-        [
-            pltpu.VMEM(prior.shape, prior.dtype),
-            pltpu.VMEM(mask.shape, mask.dtype),
-            pltpu.VMEM((mask.shape[0], edges), f32),
-            pltpu.SemaphoreType.DMA((10,)),
-        ],
-    )(place, in_hbm(mask), in_hbm(cover), in_hbm(prior))
+        [pltpu.VMEM(mask.shape[::-1], mask.dtype), pltpu.SemaphoreType.DMA((18,))],
+    )(place, in_hbm(mask.T), in_hbm(cover), in_hbm(prior))
+    here, kept_here = call(
+        own_scores_kernel,
+        [pltpu.VMEM((4 * WITH_SUMS, scen), f32), pltpu.VMEM((HALF, edges), bf16)],
+        [IN_SMEM] + [IN_VMEM] * 3,
+        [IN_VMEM] * 2,
+        2 * HALF * edges * scen,
+    )(place, in_vmem(raw), in_vmem(weights), in_vmem(rows))
+    return away, kept_away, here, kept_here
 
 
 def scores_kernel(kept_ref, weights_ref, out_ref):
@@ -120,29 +145,38 @@
     edges, scen = weights.shape
     return call(
         scores_kernel,
-        jax.ShapeDtypeStruct((HALF, scen), f32),
+        pltpu.VMEM((HALF, scen), f32),
         [IN_VMEM, IN_VMEM],
         IN_VMEM,
         2 * HALF * edges * scen,
-    )(in_vmem(kept), weights)
-
-
-def flip_kernel(own_ref, other_ref, after_ref, own_out, other_out):
+    )(in_vmem(kept), in_vmem(weights))
+
+
+def flip_kernel(place_ref, own_ref, other_ref, after_ref, own_out, other_out, zero_ref):
+    share = own_ref.shape[1] // 4
     for kept_ref, out_ref in ((own_ref, own_out), (other_ref, other_out)):
-        for d in range(4):
-            tile = kept_ref[pl.ds((4 - d) % 4 * PAIR, PAIR), :]
-            out_ref[:, d * PAIR : (d + 1) * PAIR] = tile.T
-
-
-def flip(own, other, after):
+        for e in range(4):
+            y = lax.rem(place_ref[2] + e, 4)
+            edges = pl.ds(pl.multiple_of(y * share, share), share)
+            for d in range(4):
+                tile = kept_ref[pl.ds((4 - d) % 4 * PAIR, PAIR), edges]
+                out_ref[e * share : (e + 1) * share, d * PAIR : (d + 1) * PAIR] = tile.T
+    zero_ref[...] = jnp.zeros(zero_ref.shape, f32)
+
+
+def flip(own, other, place, after):
     edges = own.shape[1]
     return call(
         flip_kernel,
-        [pltpu.VMEM((edges, HALF), bf16), pltpu.VMEM((edges, HALF), bf16)],
-        [IN_VMEM, IN_VMEM, ANYWHERE],
-        [IN_VMEM, IN_VMEM],
+        [
+            pltpu.VMEM((edges, HALF), bf16),
+            pltpu.VMEM((edges, HALF), bf16),
+            jax.ShapeDtypeStruct((8, after.shape[1]), f32),
+        ],
+        [IN_SMEM, IN_VMEM, IN_VMEM, ANYWHERE],
+        [IN_VMEM, IN_VMEM, IN_VMEM],
         16 * HALF * edges * 128,
-    )(in_vmem(own), in_vmem(other), after)
+    )(place, in_vmem(own), in_vmem(other), after)
 
 
 def column_sums(low):
@@ -167,7 +201,9 @@
 def whole_loads_kernel(flipped_ref, low_ref, load_in, size_in, load_ref, power_ref):
     load, size = add_loads(flipped_ref, low_ref, load_in[...], size_in[...])
     power = jnp.floor(jnp.log2(jnp.maximum(size, 1e-30)))
-    load_ref[...] = load * jnp.exp2(11.0 - power[:1, :])
+    share = load.shape[0] // 4
+    load_ref[:share, :] = load[:share]
+    load_ref[share:, :] = load[share:] * jnp.exp2(11.0 - power[:1, :])
     power_ref[...] = power
 
 
@@ -242,18 +278,55 @@
     return (value[:-16] + 32768.0) * jnp.exp2(value[-16:-15] - 16.0)
 
 
+def to_float16(value):
+    return lax.reduce_precision(value, 5, 10)
+
+
+def pack_part(load, power):
+    return to_float16(jnp.concatenate([load, power, power], axis=0)).astype(jnp.float16)
+
+
+def unpack_part(wire):
+    wire = wire.astype(f32)
+    return wire[:-16] * jnp.exp2(wire[-16:-15] - 11.0), wire[-16:-8]
+
+
 def pack_load(load, power, total):
+    load = load * jnp.exp2(11.0 - power[:1])
     scale = jnp.floor(jnp.log2(jnp.maximum(total, 1e-30)))
     total = total * jnp.exp2(-scale)
-    high = lax.reduce_precision(total, 5, 10)
-    wire = jnp.concatenate([load, power, scale, high, (total - high) * 1024.0], axis=0)
-    return lax.reduce_precision(wire, 5, 10)
-
-
-def unpack_load(wire):
-    wire = wire.astype(f32)
-    power, scale, high, low = (wire[at : at + 1] for at in range(wire.shape[0] - 32, wire.shape[0], 8))
-    return wire[:-32] * jnp.exp2(power - 11.0), (high + low * (1.0 / 1024.0)) * jnp.exp2(scale)
+    high = to_float16(total)
+    return to_float16(jnp.concatenate([load, power, scale, high, (total - high) * 1024.0], axis=0))
+
+
+def update_kernel(place_ref, zero, one, two, three, current_ref, out_ref, low_ref, mean_ref):
+    share = zero.shape[0] - 32
+    powers, totals = [], []
+    for wire in (zero, one, two, three):
+        power, scale, high, low = (wire[share + 8 * n : share + 8 * n + 1, :] for n in range(4))
+        powers.append(power)
+        totals.append((high + low * (1.0 / 1024.0)) * jnp.exp2(scale))
+    mean = ((totals[0] + totals[2]) + (totals[1] + totals[3])) * (1.0 / (EDGES * SCEN)) + 1e-06
+    mean_ref[...] = jnp.broadcast_to(mean, mean_ref.shape)
+    for d, wire in enumerate((zero, one, two, three)):
+        y = lax.rem(place_ref[2] + d, 4)
+        rows = pl.ds(pl.multiple_of(y * share, share), share)
+        factor = -0.25 * jnp.exp2(powers[d] - 11.0) / mean
+        new = current_ref[rows, :].astype(f32) * jnp.exp(wire[:share, :] * factor)
+        out_ref[rows, :] = new
+        low_ref[rows, :] = new.astype(bf16)
+
+
+def update(wires, current, place, last):
+    edges, scen = current.shape
+    shape = jax.ShapeDtypeStruct if last else pltpu.VMEM
+    return call(
+        update_kernel,
+        [shape((edges, scen), f32), pltpu.VMEM((edges, scen), bf16), jax.ShapeDtypeStruct((8, scen), f32)],
+        [IN_SMEM] + [IN_VMEM] * 5,
+        [IN_VMEM] * 3,
+        10**7,
+    )(place, *wires, current)
 
 
 def ring(n, d, stride=1):
@@ -264,8 +337,8 @@
     return [(i, i ^ bit) for i in range(16)]
 
 
-def shifts(value, axis):
-    return [lax.ppermute(value, axis, ring(4, d)) for d in (1, 2, 3)]
+def pair_sum(value, axis, bit):
+    return value + lax.ppermute(value, axis, [(i, i ^ bit) for i in range(4)])
 
 
 def sum_four(parts):
@@ -276,21 +349,18 @@
 def body(coverage, block_mask, edge_prior, test_cost):
     at = lax.axis_index("col")
     x, z, core = at // 4, (at // 2) % 2, at % 2
-    place = jnp.stack([x, core]).astype(jnp.int32)
-    other = jnp.stack([x, 1 - core]).astype(jnp.int32)
+    place = jnp.stack([x, core, lax.axis_index("row")]).astype(jnp.int32)
     costs = test_cost.reshape(4, 2, 2, CHUNK, test_cost.shape[1])
     cost = lax.dynamic_slice(costs, (x, 0, core, 0, 0), (1, 2, 1, CHUNK, costs.shape[-1]))
     cost = cost.reshape(PAIR, costs.shape[-1]).astype(f32)
 
-    current = edge_prior.astype(f32)
-    low_weights = edge_prior
+    current = edge_prior
     for iteration in range(ITERS):
         first = iteration == 0
         pack, unpack = (pack_sums, unpack_sums) if first else (pack_int16, unpack_int16)
         with jax.named_scope("scores"):
             if first:
-                away, kept_away = first_scores(coverage, block_mask, edge_prior, other)
-                here, kept_here = first_scores(coverage, block_mask, edge_prior, place)
+                away, kept_away, here, kept_here = first_scores(coverage, block_mask, edge_prior, place)
             else:
                 away = later_scores(kept_away, low_weights)
                 here = later_scores(kept_here, low_weights)
@@ -301,7 +371,8 @@
             scores = sum_four([here[0]] + parts)
         if first:
             with jax.named_scope("flip"):
-                flipped_here, flipped_away = flip(kept_here, kept_away, scores)
+                flipped_here, flipped_away, zero = flip(kept_here, kept_away, place, scores)
+                cost = cost + zero[:1]
         with jax.named_scope("sum_z"):
             scores = scores + unpack(lax.ppermute(pack(scores), "col", swap(2)))
             ratios = scores[:PAIR] / cost
@@ -317,20 +388,27 @@
                 sums_here, sums_away = low_here, low_away
         with jax.named_scope("total"):
             total = total_load(sums_here, sums_away, low_here, low_away)
-            total = sum_four([total] + shifts(total, "depth"))
+            total = pair_sum(pair_sum(total, "depth", 1), "depth", 2)
         with jax.named_scope("loads"):
             half, size = loads(half_loads_kernel, flipped_here, low_here)
             load, power = loads(whole_loads_kernel, flipped_away, low_away, half, size)
         with jax.named_scope("sum_y"):
-            wire = pack_load(load, power, total)
-            pairs = [unpack_load(part) for part in [wire] + shifts(wire.astype(jnp.float16), "row")]
-            edge_load = sum_four([pair[0] for pair in pairs])
-            load_mean = sum_four([pair[1] for pair in pairs]) / (EDGES * SCEN) + 1e-06
+            share = load.shape[0] // 4
+            parts, powers = [load[:share]], [power]
+            for d in (1, 2, 3):
+                wire = pack_part(load[d * share : (d + 1) * share], power)
+                part, exponent = unpack_part(lax.ppermute(wire, "row", ring(4, d)))
+                parts.append(part)
+                powers.append(exponent)
+            power = jnp.maximum(jnp.maximum(powers[0], powers[1]), jnp.maximum(powers[2], powers[3])) + 2.0
+        with jax.named_scope("gather_y"):
+            wire = pack_load(sum_four(parts), power, total)
+            sent = wire.astype(jnp.float16)
+            wires = [wire] + [lax.ppermute(sent, "row", ring(4, -d)).astype(f32) for d in (1, 2, 3)]
         with jax.named_scope("update"):
-            current = current * jnp.exp(-0.25 * edge_load / load_mean)
-            low_weights = current.astype(bf16)
+            current, low_weights, load_mean = update(wires, current, place, iteration == ITERS - 1)
     own = lax.dynamic_slice_in_dim(ratios, z * CHUNK, CHUNK, 0)
-    primal = TESTS * own / load_mean
+    primal = TESTS * own / load_mean[:1]
     return (current, primal)
 
 

time: 133 us -> 124 us (0.932)
  waiting for transfers between devices: 53.7 us -> 37.8 us
  starting transfers between devices: 47.1 us -> 55.9 us
  other arithmetic: 7.02 us -> 5.2 us
    ppermute x12 -> x16, waiting for transfers between devices: 23 us -> 8.11 us  [the longest x6 5.1 us: body(): lax.ppermute(sent, 'row', ring(4, -d)).astype(f32)]
    ppermute x12 -> x16, starting transfers between devices: 27.9 us -> 36.6 us  [the longest x4 17.6 us: pair_sum(): return value + lax.ppermute(value, axis, [(i, i ^ bit) for i in range(4)])]
    ppermute x2, waiting for transfers between devices: 5.49 us -> 3.76 us  [body(): scores = scores + unpack(lax.ppermute(pack(scores), 'col', swap(2)))]
    pallas_call x4 -> x6, Pallas kernels: 12.7 us -> 12.9 us  [the longest x1 5.97 us: first_scores(): call(first_scores_kernel, [pltpu.VMEM((4 * WITH_SUMS, scen), f32), pltpu....]
  transfers between devices with their start and end apart: 30 -> 34, of which waited for: 23 -> 21; matrix products, arithmetic and copies ran while one was open for 1% -> 1% of each run, Pallas kernels for 9% -> 7%
where the time goes in v1:
time: 124 us; the launch traced here: 123 us
  starting transfers between devices  55.9 us (45%)
  waiting for transfers between devices  37.8 us (30%)
  Pallas kernels  20.3 us (16%)
  other arithmetic  5.2 us (4%)
  local copies, waits for them, and re-layouts  1.9 us (2%)
  between operations  1.43 us (1%)
    ppermute x4, starting transfers between devices, pair_sum(): return value + lax.ppermute(value, axis, [(i, i ^ bit) for i in range(4)])  17.6 us
    ppermute x6, waiting for transfers between devices, body(): lax.ppermute(low_ratios, 'col', ring(16, d, 4))  12.1 us
    ppermute x6, waiting for transfers between devices, body(): lax.ppermute(pack(here[d]), 'col', ring(16, d, 4))  11.2 us
    ppermute x6, starting transfers between devices, body(): lax.ppermute(sent, 'row', ring(4, -d)).astype(f32)  10.1 us
    ppermute x6, starting transfers between devices, body(): lax.ppermute(pack(here[d]), 'col', ring(16, d, 4))  8.82 us
    ppermute x6, starting transfers between devices, body(): part, exponent = unpack_part(lax.ppermute(wire, 'row', ring(4, d)))  8.82 us
    ppermute x6, starting transfers between devices, body(): lax.ppermute(low_ratios, 'col', ring(16, d, 4))  6.49 us
    pallas_call x1, Pallas kernels, first_scores(): call(first_scores_kernel, [pltpu.VMEM((4 * WITH_SUMS, scen), f32), pltpu....  5.97 us
  transfers between devices with their start and end apart: 34, of which 21 were waited for; matrix products, arithmetic and copies ran while one was open for 1% of the time, Pallas kernels for 7%

profile of v1, /device:TPU:8, one launch (start us, length us, event | category | flops | bytes accessed | tf_op | source)
XLA Modules:
  0.0 122.5 jit_solution(10578544714931001099)
XLA Ops:
  0.7 6.0 %scores.4 = (f32[1568,128]{1,0:T(8,128)}, bf16[1536,1024]{1,0:T(8,128)(2,1)S(1)}, bf16[1536,1024]{1,0:T(8,128)(2,1)S(1)}, bf16[1024,128]{1,0:T(8,128)(2,1)S(1)}, f32[24,1024]{1,0:T(8,128)S(1)}) custom-call(s32[3]{0:T(128)S(1)} %pad_add_fusion.place_ref, s32[8,24]{1,0:T(8,128)} %bitcast.43, bf16[3072,1024]{1,0:T(8,128)(2,1)} %cover_ref.1, ...), custom_call_target="tpu_custom_call" | custom-call | flops 402653184 | bytes 1006632 | tf_op jit(solution)/shard_map/scores/pallas_call | solution.py:114
  6.7 1.6 %copy-done = bf16[1536,1024]{1,0:T(8,128)(2,1)} copy-done((bf16[1536,1024]{1,0:T(8,128)(2,1)}, bf16[1536,1024]{1,0:T(8,128)(2,1)S(1)}, u32[]{:S(2)}) %copy-start) | copy-done | bytes 3145752
  8.3 2.3 %scores.5 = (f32[1568,128]{1,0:T(8,128)S(1)}, bf16[1536,1024]{1,0:T(8,128)(2,1)S(1)}) custom-call(s32[3]{0:T(128)S(1)} %pad_add_fusion.place_ref, bf16[1536,1024]{1,0:T(8,128)(2,1)S(1)} %get-tuple-element.24.raw_ref, bf16[1024,128]{1,0:T(8,128)(2,1)S(1)} %get-tuple-element.25.weights_ref, f32[24,1024]{1,0:T(8,128)S(1)} %get-tuple-element.26.rows_ref), custom_call_target="tpu_custom_call" | custom-call | flops 402653184 | bytes 1006632 | tf_op jit(solution)/shard_map/scores/pallas_call | solution.py:128
  10.7 1.0 bitcast_convert_fusion
  11.6 1.4 %fusion.88 = (bf16[1568,128]{1,0:T(8,128)(2,1)S(1)}, f32[1568,128]{1,0:T(8,128)S(1)}) fusion(f32[1568,128]{1,0:T(8,128)S(1)} %get-tuple-element.29, f32[1568,128]{1,0:T(8,128)} %collective-permute-done), kind=kLoop, calls=%fused_computation.235 | loop fusion | flops 401408 | bytes 2809856 | tf_op jit(solution)/shard_map/convert.23
  13.1 3.1 %collective-permute-start.1 = (bf16[416,128]{1,0:T(8,128)(2,1)S(1)}, bf16[416,128]{1,0:T(8,128)(2,1)S(1)}, u32[]{:S(2)}, u32[]{:S(2)}) collective-permute-start(bf16[416,128]{1,0:T(8,128)(2,1)S(1)} %constant_dynamic-update-slice_fusion), channel_id=1, source_target_pairs={{0,32},{4,36},{8,40},{12,44},{16,48},{20,52},{24,56},{28,60},{32,0... | collective-permute-start | bytes 319496 | tf_op jit(solution)/shard_map/sum_x/ppermute | solution.py:370
  16.3 1.1 collective-permute-start.3
  18.3 4.2 %collective-permute-done.3 = bf16[416,128]{1,0:T(8,128)(2,1)S(1)} collective-permute-done((bf16[416,128]{1,0:T(8,128)(2,1)S(1)}, bf16[416,128]{1,0:T(8,128)(2,1)S(1)}, u32[]{:S(2)}, u32[]{:S(2)}) %collective-permute-start.3) | collective-permute-done | bytes 106528 | tf_op jit(solution)/shard_map/sum_x/ppermute | solution.py:370
  23.7 2.0 %collective-permute-start.4 = (bf16[416,128]{1,0:T(8,128)(2,1)S(1)}, bf16[416,128]{1,0:T(8,128)(2,1)S(1)}, u32[]{:S(2)}, u32[]{:S(2)}) collective-permute-start(bf16[416,128]{1,0:T(8,128)(2,1)S(1)} %constant_dynamic-update-slice_fusion.12), channel_id=1, source_target_pairs={{0,8},{4,12},{8,0},{12,4},{16,24},{20,28},{24,16},{28,20},{32,40},... | collective-permute-start | bytes 319496 | tf_op jit(solution)/shard_map/sum_z/ppermute | solution.py:377
  25.7 2.2 %flip.1 = (bf16[1024,1536]{1,0:T(8,128)(2,1)S(1)}, bf16[1024,1536]{1,0:T(8,128)(2,1)S(1)}, f32[8,128]{1,0:T(8,128)S(1)}) custom-call(s32[3]{0:T(128)S(1)} %pad_add_fusion.place_ref, bf16[1536,1024]{1,0:T(8,128)(2,1)S(1)} %get-tuple-element.27.own_ref.kept_ref, bf16[1536,1024]{1,0:T(8,128)(2,1)S(1)} %copy-done.1, f32[392,128]{1,0:T(8,128)S(1)} %fusion.4.after_ref), custom_call_target="tpu_custom_call" | custom-call | flops 3221225472 | bytes 8053063 | tf_op jit(solution)/shard_map/flip/pallas_call | solution.py:169
  28.7 2.2 %collective-permute-start.7 = (bf16[416,128]{1,0:T(8,128)(2,1)S(1)}, bf16[416,128]{1,0:T(8,128)(2,1)S(1)}, u32[]{:S(2)}, u32[]{:S(2)}) collective-permute-start(bf16[416,128]{1,0:T(8,128)(2,1)S(1)} %constant_dynamic-update-slice_fusion.16), channel_id=1, source_target_pairs={{0,48},{4,52},{8,56},{12,60},{16,0},{20,4},{24,8},{28,12},{32,16},... | collective-permute-start | bytes 319496 | tf_op jit(solution)/shard_map/gather/ppermute | solution.py:384
  32.5 6.2 %collective-permute-done.5 = bf16[416,128]{1,0:T(8,128)(2,1)S(1)} collective-permute-done((bf16[416,128]{1,0:T(8,128)(2,1)S(1)}, bf16[416,128]{1,0:T(8,128)(2,1)S(1)}, u32[]{:S(2)}, u32[]{:S(2)}) %collective-permute-start.5) | collective-permute-done | bytes 106528 | tf_op jit(solution)/shard_map/gather/ppermute | solution.py:384
  39.1 1.1 loads.4
  40.8 1.1 loads.5
  42.2 2.4 %collective-permute-start.9 = (f16[272,128]{1,0:T(8,128)(2,1)S(1)}, f16[272,128]{1,0:T(8,128)(2,1)S(1)}, u32[]{:S(2)}, u32[]{:S(2)}) collective-permute-start(f16[272,128]{1,0:T(8,128)(2,1)S(1)} %get-tuple-element.99), channel_id=1, source_target_pairs={{0,128},{64,192},{128,0},{192,64},{1,129},{65,193},{129,1},{193,65... | collective-permute-start | bytes 208904 | tf_op jit(solution)/shard_map/sum_y/ppermute | solution.py:400
  45.0 3.4 %collective-permute-start.12 = (f32[8,128]{1,0:T(8,128)S(1)}, f32[8,128]{1,0:T(8,128)S(1)}, u32[]{:S(2)}, u32[]{:S(2)}) collective-permute-start(f32[8,128]{1,0:T(8,128)S(1)} %total.2), channel_id=1, source_target_pairs={{0,1},{1,0},{2,3},{3,2},{4,5},{5,4},{6,7},{7,6},{8,9},{9,8},{10,11... | collective-permute-start | bytes 12296 | tf_op jit(solution)/shard_map/total/ppermute | solution.py:341
  48.4 1.3 %collective-permute-start.11 = (f16[272,128]{1,0:T(8,128)(2,1)S(1)}, f16[272,128]{1,0:T(8,128)(2,1)S(1)}, u32[]{:S(2)}, u32[]{:S(2)}) collective-permute-start(f16[272,128]{1,0:T(8,128)(2,1)S(1)} %get-tuple-element.100), channel_id=1, source_target_pairs={{0,192},{64,0},{128,64},{192,128},{1,193},{65,1},{129,65},{193,129... | collective-permute-start | bytes 208904 | tf_op jit(solution)/shard_map/sum_y/ppermute | solution.py:400
  50.4 6.0 %collective-permute-start.13 = (f32[8,128]{1,0:T(8,128)S(1)}, f32[8,128]{1,0:T(8,128)S(1)}, u32[]{:S(2)}, u32[]{:S(2)}) collective-permute-start(f32[8,128]{1,0:T(8,128)S(1)} %add.167), channel_id=1, source_target_pairs={{0,2},{1,3},{2,0},{3,1},{4,6},{5,7},{6,4},{7,5},{8,10},{9,11},{10,... | collective-permute-start | bytes 12296 | tf_op jit(solution)/shard_map/total/ppermute | solution.py:341
  56.7 1.4 %collective-permute-done.13 = f32[8,128]{1,0:T(8,128)S(1)} collective-permute-done((f32[8,128]{1,0:T(8,128)S(1)}, f32[8,128]{1,0:T(8,128)S(1)}, u32[]{:S(2)}, u32[]{:S(2)}) %collective-permute-start.13) | collective-permute-done | bytes 4128 | tf_op jit(solution)/shard_map/total/ppermute | solution.py:341
  58.3 3.4 %collective-permute-start.15 = (f16[288,128]{1,0:T(8,128)(2,1)S(1)}, f16[288,128]{1,0:T(8,128)(2,1)S(1)}, u32[]{:S(2)}, u32[]{:S(2)}) collective-permute-start(f16[288,128]{1,0:T(8,128)(2,1)S(1)} %get-tuple-element.92), channel_id=1, source_target_pairs={{0,128},{64,192},{128,0},{192,64},{1,129},{65,193},{129,1},{193,65... | collective-permute-start | bytes 221192 | tf_op jit(solution)/shard_map/gather_y/ppermute | solution.py:407
  61.7 1.6 %collective-permute-start.14 = (f16[288,128]{1,0:T(8,128)(2,1)S(1)}, f16[288,128]{1,0:T(8,128)(2,1)S(1)}, u32[]{:S(2)}, u32[]{:S(2)}) collective-permute-start(f16[288,128]{1,0:T(8,128)(2,1)S(1)} %get-tuple-element.92), channel_id=1, source_target_pairs={{0,192},{64,0},{128,64},{192,128},{1,193},{65,1},{129,65},{193,129... | collective-permute-start | bytes 221192 | tf_op jit(solution)/shard_map/gather_y/ppermute | solution.py:407
  63.3 0.9 collective-permute-done.15
  64.3 1.8 %collective-permute-done.14 = f16[288,128]{1,0:T(8,128)(2,1)S(1)} collective-permute-done((f16[288,128]{1,0:T(8,128)(2,1)S(1)}, f16[288,128]{1,0:T(8,128)(2,1)S(1)}, u32[]{:S(2)}, u32[]{:S(2)}) %collective-permute-start.14) | collective-permute-done | bytes 73760 | tf_op jit(solution)/shard_map/gather_y/ppermute | solution.py:407
  66.1 1.1 update.2
  67.2 1.0 scores.7
  68.3 1.0 scores.6
  69.3 1.3 %collective-permute-done.17 = f32[1536,128]{1,0:T(8,128)S(1)} collective-permute-done((f32[1536,128]{1,0:T(8,128)S(1)}, f32[1536,128]{1,0:T(8,128)S(1)}, u32[]{:S(2)}, u32[]{:S(2)}) %collective-permute-start.17) | collective-permute-done | bytes 786464 | tf_op jit(solution)/shard_map/scores/ppermute | solution.py:367
  71.1 3.3 %collective-permute-start.20 = (s16[400,128]{1,0:T(8,128)(2,1)S(1)}, s16[400,128]{1,0:T(8,128)(2,1)S(1)}, u32[]{:S(2)}, u32[]{:S(2)}) collective-permute-start(s16[400,128]{1,0:T(8,128)(2,1)S(1)} %fusion.2), channel_id=1, source_target_pairs={{0,48},{4,52},{8,56},{12,60},{16,0},{20,4},{24,8},{28,12},{32,16},... | collective-permute-start | bytes 307208 | tf_op jit(solution)/shard_map/sum_x/ppermute | solution.py:370
  74.7 2.4 %collective-permute-done.19 = s16[400,128]{1,0:T(8,128)(2,1)S(1)} collective-permute-done((s16[400,128]{1,0:T(8,128)(2,1)S(1)}, s16[400,128]{1,0:T(8,128)(2,1)S(1)}, u32[]{:S(2)}, u32[]{:S(2)}) %collective-permute-start.19) | collective-permute-done | bytes 102432 | tf_op jit(solution)/shard_map/sum_x/ppermute | solution.py:370
  77.2 1.5 %collective-permute-done.20 = s16[400,128]{1,0:T(8,128)(2,1)S(1)} collective-permute-done((s16[400,128]{1,0:T(8,128)(2,1)S(1)}, s16[400,128]{1,0:T(8,128)(2,1)S(1)}, u32[]{:S(2)}, u32[]{:S(2)}) %collective-permute-start.20) | collective-permute-done | bytes 102432 | tf_op jit(solution)/shard_map/sum_x/ppermute | solution.py:370
  78.8 2.1 %collective-permute-done.18 = s16[400,128]{1,0:T(8,128)(2,1)S(1)} collective-permute-done((s16[400,128]{1,0:T(8,128)(2,1)S(1)}, s16[400,128]{1,0:T(8,128)(2,1)S(1)}, u32[]{:S(2)}, u32[]{:S(2)}) %collective-permute-start.18) | collective-permute-done | bytes 102432 | tf_op jit(solution)/shard_map/sum_x/ppermute | solution.py:370
  81.1 1.5 %collective-permute-start.21 = (s16[400,128]{1,0:T(8,128)(2,1)S(1)}, s16[400,128]{1,0:T(8,128)(2,1)S(1)}, u32[]{:S(2)}, u32[]{:S(2)}) collective-permute-start(s16[400,128]{1,0:T(8,128)(2,1)S(1)} %fusion.3), channel_id=1, source_target_pairs={{0,8},{4,12},{8,0},{12,4},{16,24},{20,28},{24,16},{28,20},{32,40},... | collective-permute-start | bytes 307208 | tf_op jit(solution)/shard_map/sum_z/ppermute | solution.py:377
  82.6 3.2 %collective-permute-done.21 = s16[400,128]{1,0:T(8,128)(2,1)S(1)} collective-permute-done((s16[400,128]{1,0:T(8,128)(2,1)S(1)}, s16[400,128]{1,0:T(8,128)(2,1)S(1)}, u32[]{:S(2)}, u32[]{:S(2)}) %collective-permute-start.21) | collective-permute-done | bytes 102432 | tf_op jit(solution)/shard_map/sum_z/ppermute | solution.py:377
  86.0 1.7 %collective-permute-start.24 = (bf16[384,128]{1,0:T(8,128)(2,1)S(1)}, bf16[384,128]{1,0:T(8,128)(2,1)S(1)}, u32[]{:S(2)}, u32[]{:S(2)}) collective-permute-start(bf16[384,128]{1,0:T(8,128)(2,1)S(1)} %get-tuple-element.49), channel_id=1, source_target_pairs={{0,48},{4,52},{8,56},{12,60},{16,0},{20,4},{24,8},{28,12},{32,16},... | collective-permute-start | bytes 294920 | tf_op jit(solution)/shard_map/gather/ppermute | solution.py:384
  87.7 1.0 collective-permute-start.22
  88.6 2.0 %collective-permute-done.24 = bf16[384,128]{1,0:T(8,128)(2,1)S(1)} collective-permute-done((bf16[384,128]{1,0:T(8,128)(2,1)S(1)}, bf16[384,128]{1,0:T(8,128)(2,1)S(1)}, u32[]{:S(2)}, u32[]{:S(2)}) %collective-permute-start.24) | collective-permute-done | bytes 98336 | tf_op jit(solution)/shard_map/gather/ppermute | solution.py:384
  90.7 3.2 %collective-permute-done.23 = bf16[384,128]{1,0:T(8,128)(2,1)S(1)} collective-permute-done((bf16[384,128]{1,0:T(8,128)(2,1)S(1)}, bf16[384,128]{1,0:T(8,128)(2,1)S(1)}, u32[]{:S(2)}, u32[]{:S(2)}) %collective-permute-start.23) | collective-permute-done | bytes 98336 | tf_op jit(solution)/shard_map/gather/ppermute | solution.py:384
  94.7 1.0 loads.6
  96.4 1.1 loads.7
  97.7 2.4 %collective-permute-start.26 = (f16[272,128]{1,0:T(8,128)(2,1)S(1)}, f16[272,128]{1,0:T(8,128)(2,1)S(1)}, u32[]{:S(2)}, u32[]{:S(2)}) collective-permute-start(f16[272,128]{1,0:T(8,128)(2,1)S(1)} %get-tuple-element.96), channel_id=1, source_target_pairs={{0,128},{64,192},{128,0},{192,64},{1,129},{65,193},{129,1},{193,65... | collective-permute-start | bytes 208904 | tf_op jit(solution)/shard_map/sum_y/ppermute | solution.py:400
  100.6 2.4 %collective-permute-start.29 = (f32[8,128]{1,0:T(8,128)S(1)}, f32[8,128]{1,0:T(8,128)S(1)}, u32[]{:S(2)}, u32[]{:S(2)}) collective-permute-start(f32[8,128]{1,0:T(8,128)S(1)} %total.3), channel_id=1, source_target_pairs={{0,1},{1,0},{2,3},{3,2},{4,5},{5,4},{6,7},{7,6},{8,9},{9,8},{10,11... | collective-permute-start | bytes 12296 | tf_op jit(solution)/shard_map/total/ppermute | solution.py:341
  103.0 2.0 %collective-permute-start.27 = (f16[272,128]{1,0:T(8,128)(2,1)S(1)}, f16[272,128]{1,0:T(8,128)(2,1)S(1)}, u32[]{:S(2)}, u32[]{:S(2)}) collective-permute-start(f16[272,128]{1,0:T(8,128)(2,1)S(1)} %get-tuple-element.98), channel_id=1, source_target_pairs={{0,64},{64,128},{128,192},{192,0},{1,65},{65,129},{129,193},{193,1... | collective-permute-start | bytes 208904 | tf_op jit(solution)/shard_map/sum_y/ppermute | solution.py:400
  105.2 5.9 %collective-permute-start.30 = (f32[8,128]{1,0:T(8,128)S(1)}, f32[8,128]{1,0:T(8,128)S(1)}, u32[]{:S(2)}, u32[]{:S(2)}) collective-permute-start(f32[8,128]{1,0:T(8,128)S(1)} %add.182), channel_id=1, source_target_pairs={{0,2},{1,3},{2,0},{3,1},{4,6},{5,7},{6,4},{7,5},{8,10},{9,11},{10,... | collective-permute-start | bytes 12296 | tf_op jit(solution)/shard_map/total/ppermute | solution.py:341
  111.2 1.5 %collective-permute-done.30 = f32[8,128]{1,0:T(8,128)S(1)} collective-permute-done((f32[8,128]{1,0:T(8,128)S(1)}, f32[8,128]{1,0:T(8,128)S(1)}, u32[]{:S(2)}, u32[]{:S(2)}) %collective-permute-start.30) | collective-permute-done | bytes 4128 | tf_op jit(solution)/shard_map/total/ppermute | solution.py:341
  113.7 2.1 %collective-permute-start.32 = (f16[288,128]{1,0:T(8,128)(2,1)S(1)}, f16[288,128]{1,0:T(8,128)(2,1)S(1)}, u32[]{:S(2)}, u32[]{:S(2)}) collective-permute-start(f16[288,128]{1,0:T(8,128)(2,1)S(1)} %get-tuple-element.90), channel_id=1, source_target_pairs={{0,128},{64,192},{128,0},{192,64},{1,129},{65,193},{129,1},{193,65... | collective-permute-start | bytes 221192 | tf_op jit(solution)/shard_map/gather_y/ppermute | solution.py:407
  115.8 2.1 %collective-permute-start.31 = (f16[288,128]{1,0:T(8,128)(2,1)S(1)}, f16[288,128]{1,0:T(8,128)(2,1)S(1)}, u32[]{:S(2)}, u32[]{:S(2)}) collective-permute-start(f16[288,128]{1,0:T(8,128)(2,1)S(1)} %get-tuple-element.90), channel_id=1, source_target_pairs={{0,192},{64,0},{128,64},{192,128},{1,193},{65,1},{129,65},{193,129... | collective-permute-start | bytes 221192 | tf_op jit(solution)/shard_map/gather_y/ppermute | solution.py:407
  118.0 1.6 %collective-permute-done.32 = f16[288,128]{1,0:T(8,128)(2,1)S(1)} collective-permute-done((f16[288,128]{1,0:T(8,128)(2,1)S(1)}, f16[288,128]{1,0:T(8,128)(2,1)S(1)}, u32[]{:S(2)}, u32[]{:S(2)}) %collective-permute-start.32) | collective-permute-done | bytes 73760 | tf_op jit(solution)/shard_map/gather_y/ppermute | solution.py:407
  120.3 1.5 %update.3 = (f32[1024,128]{1,0:T(8,128)}, bf16[1024,128]{1,0:T(8,128)(2,1)}, f32[8,128]{1,0:T(8,128)S(1)}) custom-call(s32[3]{0:T(128)S(1)} %pad_add_fusion.place_ref, f32[288,128]{1,0:T(8,128)S(1)} %get-tuple-element.91.zero, f32[288,128]{1,0:T(8,128)S(1)} %convert_element_type.190.one, f32[288,128]{1,0:T(8,128)S(1)} %convert_element_type.191.two, ...), custom_call_target="tpu_custom_call" | custom-call | flops 10000000 | bytes 25000 | tf_op jit(solution)/shard_map/update/pallas_call | solution.py:323
  (146 shorter events, 13.4 us)
Async XLA Ops:
  6.7 1.6 %copy-start = (bf16[1536,1024]{1,0:T(8,128)(2,1)}, bf16[1536,1024]{1,0:T(8,128)(2,1)S(1)}, u32[]{:S(2)}) copy-start(bf16[1536,1024]{1,0:T(8,128)(2,1)S(1)} %get-tuple-element.28.other_ref.kept_ref) | copy-start | bytes 9437188
  8.3 3.3 %collective-permute-start = (f32[1568,128]{1,0:T(8,128)}, f32[1568,128]{1,0:T(8,128)}, u32[]{:S(2)}, u32[]{:S(2)}) collective-permute-start(f32[1568,128]{1,0:T(8,128)} %get-tuple-element.30), channel_id=1, source_target_pairs={{0,4},{4,0},{8,12},{12,8},{16,20},{20,16},{24,28},{28,24},{32,36},... | collective-permute-start | bytes 2408456 | tf_op jit(solution)/shard_map/scores/ppermute | solution.py:367
  11.6 14.1 %copy-start.1 = (bf16[1536,1024]{1,0:T(8,128)(2,1)S(1)}, bf16[1536,1024]{1,0:T(8,128)(2,1)}, u32[]{:S(2)}) copy-start(bf16[1536,1024]{1,0:T(8,128)(2,1)} %copy-done) | copy-start | bytes 9437188
  13.1 10.3 %collective-permute-start.1 = (bf16[416,128]{1,0:T(8,128)(2,1)S(1)}, bf16[416,128]{1,0:T(8,128)(2,1)S(1)}, u32[]{:S(2)}, u32[]{:S(2)}) collective-permute-start(bf16[416,128]{1,0:T(8,128)(2,1)S(1)} %constant_dynamic-update-slice_fusion), channel_id=1, source_target_pairs={{0,32},{4,36},{8,40},{12,44},{16,48},{20,52},{24,56},{28,60},{32,0... | collective-permute-start | bytes 319496 | tf_op jit(solution)/shard_map/sum_x/ppermute | solution.py:370
  16.3 6.2 %collective-permute-start.3 = (bf16[416,128]{1,0:T(8,128)(2,1)S(1)}, bf16[416,128]{1,0:T(8,128)(2,1)S(1)}, u32[]{:S(2)}, u32[]{:S(2)}) collective-permute-start(bf16[416,128]{1,0:T(8,128)(2,1)S(1)} %constant_dynamic-update-slice_fusion.8), channel_id=1, source_target_pairs={{0,48},{4,52},{8,56},{12,60},{16,0},{20,4},{24,8},{28,12},{32,16},... | collective-permute-start | bytes 319496 | tf_op jit(solution)/shard_map/sum_x/ppermute | solution.py:370
  17.4 6.0 %collective-permute-start.2 = (bf16[416,128]{1,0:T(8,128)(2,1)S(1)}, bf16[416,128]{1,0:T(8,128)(2,1)S(1)}, u32[]{:S(2)}, u32[]{:S(2)}) collective-permute-start(bf16[416,128]{1,0:T(8,128)(2,1)S(1)} %constant_dynamic-update-slice_fusion.4), channel_id=1, source_target_pairs={{0,16},{4,20},{8,24},{12,28},{16,32},{20,36},{24,40},{28,44},{32,4... | collective-permute-start | bytes 319496 | tf_op jit(solution)/shard_map/sum_x/ppermute | solution.py:370
  23.7 4.8 %collective-permute-start.4 = (bf16[416,128]{1,0:T(8,128)(2,1)S(1)}, bf16[416,128]{1,0:T(8,128)(2,1)S(1)}, u32[]{:S(2)}, u32[]{:S(2)}) collective-permute-start(bf16[416,128]{1,0:T(8,128)(2,1)S(1)} %constant_dynamic-update-slice_fusion.12), channel_id=1, source_target_pairs={{0,8},{4,12},{8,0},{12,4},{16,24},{20,28},{24,16},{28,20},{32,40},... | collective-permute-start | bytes 319496 | tf_op jit(solution)/shard_map/sum_z/ppermute | solution.py:377
  28.7 10.1 %collective-permute-start.7 = (bf16[416,128]{1,0:T(8,128)(2,1)S(1)}, bf16[416,128]{1,0:T(8,128)(2,1)S(1)}, u32[]{:S(2)}, u32[]{:S(2)}) collective-permute-start(bf16[416,128]{1,0:T(8,128)(2,1)S(1)} %constant_dynamic-update-slice_fusion.16), channel_id=1, source_target_pairs={{0,48},{4,52},{8,56},{12,60},{16,0},{20,4},{24,8},{28,12},{32,16},... | collective-permute-start | bytes 319496 | tf_op jit(solution)/shard_map/gather/ppermute | solution.py:384
  30.9 7.8 %collective-permute-start.6 = (bf16[416,128]{1,0:T(8,128)(2,1)S(1)}, bf16[416,128]{1,0:T(8,128)(2,1)S(1)}, u32[]{:S(2)}, u32[]{:S(2)}) collective-permute-start(bf16[416,128]{1,0:T(8,128)(2,1)S(1)} %constant_dynamic-update-slice_fusion.16), channel_id=1, source_target_pairs={{0,32},{4,36},{8,40},{12,44},{16,48},{20,52},{24,56},{28,60},{32,0... | collective-permute-start | bytes 319496 | tf_op jit(solution)/shard_map/gather/ppermute | solution.py:384
  31.7 7.0 %collective-permute-start.5 = (bf16[416,128]{1,0:T(8,128)(2,1)S(1)}, bf16[416,128]{1,0:T(8,128)(2,1)S(1)}, u32[]{:S(2)}, u32[]{:S(2)}) collective-permute-start(bf16[416,128]{1,0:T(8,128)(2,1)S(1)} %constant_dynamic-update-slice_fusion.16), channel_id=1, source_target_pairs={{0,16},{4,20},{8,24},{12,28},{16,32},{20,36},{24,40},{28,44},{32,4... | collective-permute-start | bytes 319496 | tf_op jit(solution)/shard_map/gather/ppermute | solution.py:384
  38.8 2.0 %collective-permute-start.8 = (bf16[1664,128]{1,0:T(8,128)(2,1)S(1)}, bf16[1664,128]{1,0:T(8,128)(2,1)S(1)}, u32[]{:S(2)}, u32[]{:S(2)}) collective-permute-start(bf16[1664,128]{1,0:T(8,128)(2,1)S(1)} %constant_dynamic-update-slice_fusion.21.low_ref.sums_own.low_own), channel_id=1, source_target_pairs={{0,4},{4,0},{8,12},{12,8},{16,20},{20,16},{24,28},{28,24},{32,36},... | collective-permute-start | bytes 1277960 | tf_op jit(solution)/shard_map/gather/ppermute | solution.py:386
  41.9 24.1 %copy-start.2 = (bf16[1024,128]{1,0:T(8,128)(2,1)S(1)}, bf16[1024,128]{1,0:T(8,128)(2,1)}, u32[]{:S(2)}) copy-start(bf16[1024,128]{1,0:T(8,128)(2,1)} %current_ref.1) | copy-start | bytes 786436
  42.2 14.2 %collective-permute-start.9 = (f16[272,128]{1,0:T(8,128)(2,1)S(1)}, f16[272,128]{1,0:T(8,128)(2,1)S(1)}, u32[]{:S(2)}, u32[]{:S(2)}) collective-permute-start(f16[272,128]{1,0:T(8,128)(2,1)S(1)} %get-tuple-element.99), channel_id=1, source_target_pairs={{0,128},{64,192},{128,0},{192,64},{1,129},{65,193},{129,1},{193,65... | collective-permute-start | bytes 208904 | tf_op jit(solution)/shard_map/sum_y/ppermute | solution.py:400
  45.0 5.4 %collective-permute-start.12 = (f32[8,128]{1,0:T(8,128)S(1)}, f32[8,128]{1,0:T(8,128)S(1)}, u32[]{:S(2)}, u32[]{:S(2)}) collective-permute-start(f32[8,128]{1,0:T(8,128)S(1)} %total.2), channel_id=1, source_target_pairs={{0,1},{1,0},{2,3},{3,2},{4,5},{5,4},{6,7},{7,6},{8,9},{9,8},{10,11... | collective-permute-start | bytes 12296 | tf_op jit(solution)/shard_map/total/ppermute | solution.py:341
  48.4 8.1 %collective-permute-start.11 = (f16[272,128]{1,0:T(8,128)(2,1)S(1)}, f16[272,128]{1,0:T(8,128)(2,1)S(1)}, u32[]{:S(2)}, u32[]{:S(2)}) collective-permute-start(f16[272,128]{1,0:T(8,128)(2,1)S(1)} %get-tuple-element.100), channel_id=1, source_target_pairs={{0,192},{64,0},{128,64},{192,128},{1,193},{65,1},{129,65},{193,129... | collective-permute-start | bytes 208904 | tf_op jit(solution)/shard_map/sum_y/ppermute | solution.py:400
  49.8 6.8 %collective-permute-start.10 = (f16[272,128]{1,0:T(8,128)(2,1)S(1)}, f16[272,128]{1,0:T(8,128)(2,1)S(1)}, u32[]{:S(2)}, u32[]{:S(2)}) collective-permute-start(f16[272,128]{1,0:T(8,128)(2,1)S(1)} %get-tuple-element.101), channel_id=1, source_target_pairs={{0,64},{64,128},{128,192},{192,0},{1,65},{65,129},{129,193},{193,1... | collective-permute-start | bytes 208904 | tf_op jit(solution)/shard_map/sum_y/ppermute | solution.py:400
  50.4 7.6 %collective-permute-start.13 = (f32[8,128]{1,0:T(8,128)S(1)}, f32[8,128]{1,0:T(8,128)S(1)}, u32[]{:S(2)}, u32[]{:S(2)}) collective-permute-start(f32[8,128]{1,0:T(8,128)S(1)} %add.167), channel_id=1, source_target_pairs={{0,2},{1,3},{2,0},{3,1},{4,6},{5,7},{6,4},{7,5},{8,10},{9,11},{10,... | collective-permute-start | bytes 12296 | tf_op jit(solution)/shard_map/total/ppermute | solution.py:341
  58.2 5.1 %collective-permute-start.16 = (f16[288,128]{1,0:T(8,128)(2,1)S(1)}, f16[288,128]{1,0:T(8,128)(2,1)S(1)}, u32[]{:S(2)}, u32[]{:S(2)}) collective-permute-start(f16[288,128]{1,0:T(8,128)(2,1)S(1)} %get-tuple-element.92), channel_id=1, source_target_pairs={{0,64},{64,128},{128,192},{192,0},{1,65},{65,129},{129,193},{193,1... | collective-permute-start | bytes 221192 | tf_op jit(solution)/shard_map/gather_y/ppermute | solution.py:407
  58.3 5.9 %collective-permute-start.15 = (f16[288,128]{1,0:T(8,128)(2,1)S(1)}, f16[288,128]{1,0:T(8,128)(2,1)S(1)}, u32[]{:S(2)}, u32[]{:S(2)}) collective-permute-start(f16[288,128]{1,0:T(8,128)(2,1)S(1)} %get-tuple-element.92), channel_id=1, source_target_pairs={{0,128},{64,192},{128,0},{192,64},{1,129},{65,193},{129,1},{193,65... | collective-permute-start | bytes 221192 | tf_op jit(solution)/shard_map/gather_y/ppermute | solution.py:407
  61.7 4.4 %collective-permute-start.14 = (f16[288,128]{1,0:T(8,128)(2,1)S(1)}, f16[288,128]{1,0:T(8,128)(2,1)S(1)}, u32[]{:S(2)}, u32[]{:S(2)}) collective-permute-start(f16[288,128]{1,0:T(8,128)(2,1)S(1)} %get-tuple-element.92), channel_id=1, source_target_pairs={{0,192},{64,0},{128,64},{192,128},{1,193},{65,1},{129,65},{193,129... | collective-permute-start | bytes 221192 | tf_op jit(solution)/shard_map/gather_y/ppermute | solution.py:407
  68.2 2.4 %collective-permute-start.17 = (f32[1536,128]{1,0:T(8,128)S(1)}, f32[1536,128]{1,0:T(8,128)S(1)}, u32[]{:S(2)}, u32[]{:S(2)}) collective-permute-start(f32[1536,128]{1,0:T(8,128)S(1)} %scores.7), channel_id=1, source_target_pairs={{0,4},{4,0},{8,12},{12,8},{16,20},{20,16},{24,28},{28,24},{32,36},... | collective-permute-start | bytes 2359304 | tf_op jit(solution)/shard_map/scores/ppermute | solution.py:367
  70.9 6.2 %collective-permute-start.19 = (s16[400,128]{1,0:T(8,128)(2,1)S(1)}, s16[400,128]{1,0:T(8,128)(2,1)S(1)}, u32[]{:S(2)}, u32[]{:S(2)}) collective-permute-start(s16[400,128]{1,0:T(8,128)(2,1)S(1)} %fusion.1), channel_id=1, source_target_pairs={{0,16},{4,20},{8,24},{12,28},{16,32},{20,36},{24,40},{28,44},{32,4... | collective-permute-start | bytes 307208 | tf_op jit(solution)/shard_map/sum_x/ppermute | solution.py:370
  71.1 7.6 %collective-permute-start.20 = (s16[400,128]{1,0:T(8,128)(2,1)S(1)}, s16[400,128]{1,0:T(8,128)(2,1)S(1)}, u32[]{:S(2)}, u32[]{:S(2)}) collective-permute-start(s16[400,128]{1,0:T(8,128)(2,1)S(1)} %fusion.2), channel_id=1, source_target_pairs={{0,48},{4,52},{8,56},{12,60},{16,0},{20,4},{24,8},{28,12},{32,16},... | collective-permute-start | bytes 307208 | tf_op jit(solution)/shard_map/sum_x/ppermute | solution.py:370
  74.4 6.5 %collective-permute-start.18 = (s16[400,128]{1,0:T(8,128)(2,1)S(1)}, s16[400,128]{1,0:T(8,128)(2,1)S(1)}, u32[]{:S(2)}, u32[]{:S(2)}) collective-permute-start(s16[400,128]{1,0:T(8,128)(2,1)S(1)} %fusion), channel_id=1, source_target_pairs={{0,32},{4,36},{8,40},{12,44},{16,48},{20,52},{24,56},{28,60},{32,0... | collective-permute-start | bytes 307208 | tf_op jit(solution)/shard_map/sum_x/ppermute | solution.py:370
  81.1 4.7 %collective-permute-start.21 = (s16[400,128]{1,0:T(8,128)(2,1)S(1)}, s16[400,128]{1,0:T(8,128)(2,1)S(1)}, u32[]{:S(2)}, u32[]{:S(2)}) collective-permute-start(s16[400,128]{1,0:T(8,128)(2,1)S(1)} %fusion.3), channel_id=1, source_target_pairs={{0,8},{4,12},{8,0},{12,4},{16,24},{20,28},{24,16},{28,20},{32,40},... | collective-permute-start | bytes 307208 | tf_op jit(solution)/shard_map/sum_z/ppermute | solution.py:377
  86.0 4.7 %collective-permute-start.24 = (bf16[384,128]{1,0:T(8,128)(2,1)S(1)}, bf16[384,128]{1,0:T(8,128)(2,1)S(1)}, u32[]{:S(2)}, u32[]{:S(2)}) collective-permute-start(bf16[384,128]{1,0:T(8,128)(2,1)S(1)} %get-tuple-element.49), channel_id=1, source_target_pairs={{0,48},{4,52},{8,56},{12,60},{16,0},{20,4},{24,8},{28,12},{32,16},... | collective-permute-start | bytes 294920 | tf_op jit(solution)/shard_map/gather/ppermute | solution.py:384
  87.7 6.2 %collective-permute-start.23 = (bf16[384,128]{1,0:T(8,128)(2,1)S(1)}, bf16[384,128]{1,0:T(8,128)(2,1)S(1)}, u32[]{:S(2)}, u32[]{:S(2)}) collective-permute-start(bf16[384,128]{1,0:T(8,128)(2,1)S(1)} %get-tuple-element.49), channel_id=1, source_target_pairs={{0,32},{4,36},{8,40},{12,44},{16,48},{20,52},{24,56},{28,60},{32,0... | collective-permute-start | bytes 294920 | tf_op jit(solution)/shard_map/gather/ppermute | solution.py:384
  87.7 6.9 %collective-permute-start.22 = (bf16[384,128]{1,0:T(8,128)(2,1)S(1)}, bf16[384,128]{1,0:T(8,128)(2,1)S(1)}, u32[]{:S(2)}, u32[]{:S(2)}) collective-permute-start(bf16[384,128]{1,0:T(8,128)(2,1)S(1)} %get-tuple-element.49), channel_id=1, source_target_pairs={{0,16},{4,20},{8,24},{12,28},{16,32},{20,36},{24,40},{28,44},{32,4... | collective-permute-start | bytes 294920 | tf_op jit(solution)/shard_map/gather/ppermute | solution.py:384
  94.6 1.8 %collective-permute-start.25 = (bf16[1536,128]{1,0:T(8,128)(2,1)S(1)}, bf16[1536,128]{1,0:T(8,128)(2,1)S(1)}, u32[]{:S(2)}, u32[]{:S(2)}) collective-permute-start(bf16[1536,128]{1,0:T(8,128)(2,1)S(1)} %pad_maximum_fusion.low_ref.low_own), channel_id=1, source_target_pairs={{0,4},{4,0},{8,12},{12,8},{16,20},{20,16},{24,28},{28,24},{32,36},... | collective-permute-start | bytes 1179656 | tf_op jit(solution)/shard_map/gather/ppermute | solution.py:386
  97.7 13.3 %collective-permute-start.26 = (f16[272,128]{1,0:T(8,128)(2,1)S(1)}, f16[272,128]{1,0:T(8,128)(2,1)S(1)}, u32[]{:S(2)}, u32[]{:S(2)}) collective-permute-start(f16[272,128]{1,0:T(8,128)(2,1)S(1)} %get-tuple-element.96), channel_id=1, source_target_pairs={{0,128},{64,192},{128,0},{192,64},{1,129},{65,193},{129,1},{193,65... | collective-permute-start | bytes 208904 | tf_op jit(solution)/shard_map/sum_y/ppermute | solution.py:400
  100.6 4.6 %collective-permute-start.29 = (f32[8,128]{1,0:T(8,128)S(1)}, f32[8,128]{1,0:T(8,128)S(1)}, u32[]{:S(2)}, u32[]{:S(2)}) collective-permute-start(f32[8,128]{1,0:T(8,128)S(1)} %total.3), channel_id=1, source_target_pairs={{0,1},{1,0},{2,3},{3,2},{4,5},{5,4},{6,7},{7,6},{8,9},{9,8},{10,11... | collective-permute-start | bytes 12296 | tf_op jit(solution)/shard_map/total/ppermute | solution.py:341
  103.0 8.1 %collective-permute-start.28 = (f16[272,128]{1,0:T(8,128)(2,1)S(1)}, f16[272,128]{1,0:T(8,128)(2,1)S(1)}, u32[]{:S(2)}, u32[]{:S(2)}) collective-permute-start(f16[272,128]{1,0:T(8,128)(2,1)S(1)} %get-tuple-element.97), channel_id=1, source_target_pairs={{0,192},{64,0},{128,64},{192,128},{1,193},{65,1},{129,65},{193,129... | collective-permute-start | bytes 208904 | tf_op jit(solution)/shard_map/sum_y/ppermute | solution.py:400
  103.0 8.1 %collective-permute-start.27 = (f16[272,128]{1,0:T(8,128)(2,1)S(1)}, f16[272,128]{1,0:T(8,128)(2,1)S(1)}, u32[]{:S(2)}, u32[]{:S(2)}) collective-permute-start(f16[272,128]{1,0:T(8,128)(2,1)S(1)} %get-tuple-element.98), channel_id=1, source_target_pairs={{0,64},{64,128},{128,192},{192,0},{1,65},{65,129},{129,193},{193,1... | collective-permute-start | bytes 208904 | tf_op jit(solution)/shard_map/sum_y/ppermute | solution.py:400
  105.2 7.5 %collective-permute-start.30 = (f32[8,128]{1,0:T(8,128)S(1)}, f32[8,128]{1,0:T(8,128)S(1)}, u32[]{:S(2)}, u32[]{:S(2)}) collective-permute-start(f32[8,128]{1,0:T(8,128)S(1)} %add.182), channel_id=1, source_target_pairs={{0,2},{1,3},{2,0},{3,1},{4,6},{5,7},{6,4},{7,5},{8,10},{9,11},{10,... | collective-permute-start | bytes 12296 | tf_op jit(solution)/shard_map/total/ppermute | solution.py:341
  112.9 5.1 %collective-permute-start.33 = (f16[288,128]{1,0:T(8,128)(2,1)S(1)}, f16[288,128]{1,0:T(8,128)(2,1)S(1)}, u32[]{:S(2)}, u32[]{:S(2)}) collective-permute-start(f16[288,128]{1,0:T(8,128)(2,1)S(1)} %get-tuple-element.90), channel_id=1, source_target_pairs={{0,64},{64,128},{128,192},{192,0},{1,65},{65,129},{129,193},{193,1... | collective-permute-start | bytes 221192 | tf_op jit(solution)/shard_map/gather_y/ppermute | solution.py:407
  113.7 5.9 %collective-permute-start.32 = (f16[288,128]{1,0:T(8,128)(2,1)S(1)}, f16[288,128]{1,0:T(8,128)(2,1)S(1)}, u32[]{:S(2)}, u32[]{:S(2)}) collective-permute-start(f16[288,128]{1,0:T(8,128)(2,1)S(1)} %get-tuple-element.90), channel_id=1, source_target_pairs={{0,128},{64,192},{128,0},{192,64},{1,129},{65,193},{129,1},{193,65... | collective-permute-start | bytes 221192 | tf_op jit(solution)/shard_map/gather_y/ppermute | solution.py:407
  115.8 4.5 %collective-permute-start.31 = (f16[288,128]{1,0:T(8,128)(2,1)S(1)}, f16[288,128]{1,0:T(8,128)(2,1)S(1)}, u32[]{:S(2)}, u32[]{:S(2)}) collective-permute-start(f16[288,128]{1,0:T(8,128)(2,1)S(1)} %get-tuple-element.90), channel_id=1, source_target_pairs={{0,192},{64,0},{128,64},{192,128},{1,193},{65,1},{129,65},{193,129... | collective-permute-start | bytes 221192 | tf_op jit(solution)/shard_map/gather_y/ppermute | solution.py:407

commit v2 on v1

v2 whole, which is shorter than its diff:
```python
import functools

import jax
import jax.numpy as jnp
from jax import lax
from jax.experimental import pallas as pl
from jax.experimental.pallas import tpu as pltpu
from jax.sharding import PartitionSpec as P

EDGES = 16384
SCEN = 512
BLOCK = 128
ITERS = 2
TESTS = 12288
CHUNK = 192
PAIR = 2 * CHUNK
HALF = 4 * PAIR
WITH_SUMS = PAIR + 8
GATHERED = PAIR + 32
VMEM_LIMIT = 16 * 1024 * 1024
IN_VMEM = pl.BlockSpec(memory_space=pltpu.VMEM)
IN_SMEM = pl.BlockSpec(memory_space=pltpu.SMEM)
ANYWHERE = pl.BlockSpec(memory_space=pl.ANY)
IN_HBM = pl.BlockSpec(memory_space=pltpu.HBM)
f32 = jnp.float32
bf16 = jnp.bfloat16


def call(kernel, out_shape, in_specs, out_specs, flops, scratch=()):
    return pl.pallas_call(
        kernel,
        in_specs=in_specs,
        out_specs=out_specs,
        out_shape=out_shape,
        scratch_shapes=list(scratch),
        compiler_params=pltpu.CompilerParams(vmem_limit_bytes=VMEM_LIMIT),
        cost_estimate=pl.CostEstimate(flops=flops, bytes_accessed=flops // 400, transcendentals=0),
    )


def in_vmem(value):
    return pltpu.with_memory_space_constraint(value, pltpu.VMEM)


def in_hbm(value):
    return pltpu.with_memory_space_constraint(value, pltpu.HBM)


def tests_of(kept_ref, d, core, edges=slice(None)):
    at = [pl.multiple_of((d * 4 + z * 2 + core) * CHUNK, CHUNK) for z in range(2)]
    return jnp.concatenate([kept_ref[pl.ds(a, CHUNK), edges] for a in at], axis=0)


def scores_and_sums(kept, weights, out_ref, d):
    at = d * WITH_SUMS
    out_ref[at : at + PAIR, :] = jnp.dot(kept, weights, preferred_element_type=f32)
    ones = jnp.ones((8, kept.shape[1]), bf16)
    sums = lax.dot_general(ones, kept, (((1,), (1,)), ((), ())), preferred_element_type=f32)
    out_ref[at + PAIR : at + WITH_SUMS, :] = jnp.concatenate(
        [sums[:1, j * BLOCK : (j + 1) * BLOCK] for j in range(3)] + [jnp.zeros((5, BLOCK), f32)], axis=0
    )


def first_scores_kernel(place_ref, mask_ref, cover_ref, prior_ref, out_ref, kept_ref, weights_ref, rows_ref, tiles_ref, sems):
    tiles = pltpu.make_async_copy(mask_ref, tiles_ref, sems.at[4])
    tiles.start()
    copies = []
    for d in range(4):
        rows = pl.ds(pl.multiple_of(lax.rem(place_ref[0] + d, 4) * 4 * CHUNK, CHUNK), 4 * CHUNK)
        copy = pltpu.make_async_copy(
            cover_ref.at[rows, :], kept_ref.at[pl.ds(d * 4 * CHUNK, 4 * CHUNK), :], sems.at[d]
        )
        copy.start()
        copies.append(copy)
        if d == 0:
            weights = pltpu.make_async_copy(prior_ref, weights_ref, sems.at[5])
            weights.start()
    edges = cover_ref.shape[1]
    tiles.wait()
    column = lax.broadcasted_iota(jnp.int32, (tiles_ref.shape[0], edges), 1) // BLOCK
    spread = column == lax.broadcasted_iota(jnp.int32, column.shape, 0)
    rows_ref[...] = lax.dot_general(
        tiles_ref[...].astype(f32), spread.astype(f32), (((0,), (0,)), ((), ())), preferred_element_type=f32
    )
    weights.wait()
    blocks = 4 * CHUNK // BLOCK
    for d in range(4):
        copies[d].wait()
        first = lax.rem(place_ref[0] + d, 4) * blocks
        for b in range(blocks):
            entry = jnp.broadcast_to(rows_ref[pl.ds(first + b, 1), :], (16, edges)).astype(bf16)
            for k in range(BLOCK // 16):
                at = (d * blocks + b) * BLOCK + k * 16
                kept_ref[at : at + 16, :] = kept_ref[at : at + 16, :] * entry
        scores_and_sums(tests_of(kept_ref, d, 1 - place_ref[1]), weights_ref[...], out_ref, d)


def own_scores_kernel(place_ref, kept_ref, weights_ref, out_ref):
    for d in range(4):
        scores_and_sums(tests_of(kept_ref, d, place_ref[1]), weights_ref[...], out_ref, d)


def first_scores(cover, mask, prior, place):
    edges, scen = prior.shape
    away, kept, weights = call(
        first_scores_kernel,
        [
            pltpu.VMEM((4 * WITH_SUMS, scen), f32),
            pltpu.VMEM(cover.shape, bf16),
            pltpu.VMEM(prior.shape, bf16),
        ],
        [IN_SMEM, IN_HBM, IN_HBM, IN_HBM],
        [IN_VMEM] * 3,
        2 * HALF * edges * scen,
        [
            pltpu.VMEM((mask.shape[0], edges), f32),
            pltpu.VMEM(mask.shape[::-1], mask.dtype),
            pltpu.SemaphoreType.DMA((6,)),
        ],
    )(place, in_hbm(mask.T), in_hbm(cover), in_hbm(prior))
    here = call(
        own_scores_kernel,
        pltpu.VMEM((4 * WITH_SUMS, scen), f32),
        [IN_SMEM, IN_VMEM, IN_VMEM],
        IN_VMEM,
        2 * HALF * edges * scen,
    )(place, in_vmem(kept), in_vmem(weights))
    return away, here, kept, weights


def scores_kernel(own, place_ref, kept_ref, weights_ref, out_ref):
    core = place_ref[1] if own else 1 - place_ref[1]
    for d in range(4):
        out_ref[d * PAIR : (d + 1) * PAIR, :] = jnp.dot(
            tests_of(kept_ref, d, core), weights_ref[...], preferred_element_type=f32
        )


def later_scores(own, kept, weights, place):
    edges, scen = weights.shape
    return call(
        functools.partial(scores_kernel, own),
        pltpu.VMEM((HALF, scen), f32),
        [IN_SMEM, IN_VMEM, IN_VMEM],
        IN_VMEM,
        2 * HALF * edges * scen,
    )(place, in_vmem(kept), in_vmem(weights))


def flip_kernel(place_ref, kept_ref, cost_ref, after_ref, own_out, other_out, cost_out, cost_in, sems):
    copies = []
    for z in range(2):
        at = pl.multiple_of((place_ref[0] * 4 + z * 2 + place_ref[1]) * CHUNK, CHUNK)
        copy = pltpu.make_async_copy(
            cost_ref.at[pl.ds(at, CHUNK), :], cost_in.at[pl.ds(z * CHUNK, CHUNK), :], sems.at[z]
        )
        copy.start()
        copies.append(copy)
    share = kept_ref.shape[1] // 4
    for half, out_ref in enumerate((own_out, other_out)):
        core = 1 - place_ref[1] if half else place_ref[1]
        for e in range(4):
            y = lax.rem(place_ref[2] + e, 4)
            edges = pl.ds(pl.multiple_of(y * share, share), share)
            for d in range(4):
                tile = tests_of(kept_ref, (4 - d) % 4, core, edges)
                out_ref[e * share : (e + 1) * share, d * PAIR : (d + 1) * PAIR] = tile.T
    for copy in copies:
        copy.wait()
    cost_out[...] = cost_in[...].astype(f32)


def flip(kept, cost, place, after):
    edges = kept.shape[1]
    return call(
        flip_kernel,
        [
            pltpu.VMEM((edges, HALF), bf16),
            pltpu.VMEM((edges, HALF), bf16),
            pltpu.VMEM((PAIR, cost.shape[1]), f32),
        ],
        [IN_SMEM, IN_VMEM, IN_HBM, ANYWHERE],
        [IN_VMEM, IN_VMEM, IN_VMEM],
        16 * HALF * edges * 128,
        [pltpu.VMEM((PAIR, cost.shape[1]), cost.dtype), pltpu.SemaphoreType.DMA((2,))],
    )(place, in_vmem(kept), in_hbm(cost), after)


def column_sums(low):
    return jnp.dot(jnp.ones((8, low.shape[0]), bf16), low, preferred_element_type=f32)


def add_loads(flipped_ref, low_ref, load, size):
    stride = low_ref.shape[0] // 4
    for d in range(4):
        low = low_ref[d * stride : d * stride + PAIR, :]
        load += jnp.dot(flipped_ref[:, d * PAIR : (d + 1) * PAIR], low, preferred_element_type=f32)
        size += column_sums(low)
    return load, size


def half_loads_kernel(flipped_ref, low_ref, load_ref, size_ref):
    load, size = add_loads(flipped_ref, low_ref, jnp.zeros(load_ref.shape, f32), jnp.zeros(size_ref.shape, f32))
    load_ref[...] = load
    size_ref[...] = size


def whole_loads_kernel(flipped_ref, low_ref, load_in, size_in, load_ref, power_ref):
    load, size = add_loads(flipped_ref, low_ref, load_in[...], size_in[...])
    power = jnp.floor(jnp.log2(jnp.maximum(size, 1e-30)))
    share = load.shape[0] // 4
    load_ref[:share, :] = load[:share]
    load_ref[share:, :] = load[share:] * jnp.exp2(11.0 - power[:1, :])
    power_ref[...] = power


def loads(kernel, flipped, low, *so_far):
    edges, scen = flipped.shape[0], low.shape[1]
    return call(
        kernel,
        [jax.ShapeDtypeStruct((edges, scen), f32), jax.ShapeDtypeStruct((8, scen), f32)],
        [IN_VMEM] * (2 + len(so_far)),
        [IN_VMEM, IN_VMEM],
        2 * HALF * edges * scen,
    )(in_vmem(flipped), low, *so_far)


def total_kernel(sums_own, sums_away, low_own, low_away, out_ref):
    totals = [jnp.zeros((32, BLOCK), f32) for _ in range(3)]
    stride = low_own.shape[0] // 4
    for sums_ref, low_ref in ((sums_own, low_own), (sums_away, low_away)):
        for d in range(4):
            sums = sums_ref[d * GATHERED + PAIR : (d + 1) * GATHERED, :]
            for j in range(3):
                low = low_ref[d * stride + j * BLOCK : d * stride + (j + 1) * BLOCK, :]
                totals[j] += jnp.dot(sums, low, preferred_element_type=f32)
    row = lax.broadcasted_iota(jnp.int32, (32, BLOCK), 0)
    total = jnp.zeros((32, BLOCK), f32)
    for j in range(3):
        total += jnp.where(row % 8 == j, totals[j], 0.0)
    out_ref[...] = jnp.full(out_ref.shape, jnp.sum(total), f32)


def total_load(sums_own, sums_away, low_own, low_away):
    return call(
        total_kernel,
        jax.ShapeDtypeStruct((8, low_own.shape[1]), f32),
        [IN_VMEM] * 4,
        IN_VMEM,
        10**8,
    )(sums_own, sums_away, low_own, low_away)


def bf16_parts(sums):
    parts = []
    left = sums
    for _ in range(3):
        part = lax.reduce_precision(left, 8, 7)
        left = left - part
        parts.append(part)
    return parts + [jnp.zeros_like(sums)]


def pack_sums(value):
    return jnp.concatenate([value[:PAIR]] + bf16_parts(value[PAIR:]), axis=0).astype(bf16)


def unpack_sums(value):
    value = value.astype(f32)
    sums = value[PAIR : PAIR + 8] + value[PAIR + 8 : PAIR + 16] + value[PAIR + 16 : PAIR + 24]
    return jnp.concatenate([value[:PAIR], sums], axis=0)


def pack_int16(value):
    top = jnp.max(value, axis=0, keepdims=True)
    power = jnp.ceil(jnp.log2(jnp.maximum(top, 1e-30)))
    code = jnp.round(value * jnp.exp2(16.0 - power)) - 32768.0
    code = jnp.clip(code, -32768.0, 32767.0)
    tile = jnp.broadcast_to(power, (16, value.shape[1]))
    return jnp.concatenate([code, tile], axis=0).astype(jnp.int32).astype(jnp.int16)


def unpack_int16(value):
    value = value.astype(jnp.int32).astype(f32)
    return (value[:-16] + 32768.0) * jnp.exp2(value[-16:-15] - 16.0)


def to_float16(value):
    return lax.reduce_precision(value, 5, 10)


def pack_part(load, power, total):
    return jnp.concatenate([load, power] + total, axis=0).astype(jnp.float16)


def float16_parts(total):
    scale = jnp.floor(jnp.log2(jnp.maximum(total, 1e-30)))
    total = total * jnp.exp2(-scale)
    high = to_float16(total)
    return [scale, high, to_float16((total - high) * 1024.0)]


def from_parts(scale, high, low):
    return (high + low * (1.0 / 1024.0)) * jnp.exp2(scale)


def unpack_part(wire):
    wire = wire.astype(f32)
    share = wire.shape[0] - 32
    power, *total = (wire[at : at + 8] for at in range(share, share + 32, 8))
    return wire[:share] * jnp.exp2(power[:1] - 11.0), power, from_parts(*total)


def pack_load(load, power):
    return to_float16(jnp.concatenate([load * jnp.exp2(11.0 - power[:1]), power, power], axis=0))


def update_kernel(last, place_ref, zero, one, two, three, total_ref, current_ref, *rest):
    share = zero.shape[0] - 16
    mean = total_ref[:1, :] * (1.0 / (EDGES * SCEN)) + 1e-06
    if last:
        ratios_ref, out_ref, primal_ref = rest
        own = ratios_ref[pl.ds(pl.multiple_of(place_ref[3] * CHUNK, CHUNK), CHUNK), :]
        primal_ref[...] = TESTS * own / mean
    else:
        out_ref, low_ref = rest
    for d, wire in enumerate((zero, one, two, three)):
        y = lax.rem(place_ref[2] + d, 4)
        rows = pl.ds(pl.multiple_of(y * share, share), share)
        factor = -0.25 * jnp.exp2(wire[share : share + 1, :] - 11.0) / mean
        new = current_ref[rows, :].astype(f32) * jnp.exp(wire[:share, :] * factor)
        out_ref[rows, :] = new
        if not last:
            low_ref[rows, :] = new.astype(bf16)


def update(wires, total, current, place, ratios=None):
    edges, scen = current.shape
    last = ratios is not None
    if last:
        shapes = [jax.ShapeDtypeStruct((edges, scen), f32), jax.ShapeDtypeStruct((CHUNK, scen), f32)]
    else:
        shapes = [pltpu.VMEM((edges, scen), f32), pltpu.VMEM((edges, scen), bf16)]
    return call(
        functools.partial(update_kernel, last),
        shapes,
        [IN_SMEM] + [IN_VMEM] * (7 if last else 6),
        [IN_VMEM] * 2,
        10**7,
    )(place, *wires, total, in_vmem(current), *([ratios] if last else []))


def ring(n, d, stride=1):
    return [(i, (i + d * stride) % n) for i in range(n)]


def swap(bit):
    return [(i, i ^ bit) for i in range(16)]


def pair_sum(value, axis, bit):
    return value + lax.ppermute(value, axis, [(i, i ^ bit) for i in range(4)])


def sum_four(parts):
    zero, one, two, three = parts
    return (zero + two) + (one + three)


def body(coverage, block_mask, edge_prior, test_cost):
    at = lax.axis_index("col")
    x, z, core = at // 4, (at // 2) % 2, at % 2
    place = jnp.stack([x, core, lax.axis_index("row"), z]).astype(jnp.int32)
    for iteration in range(ITERS):
        first = iteration == 0
        pack, unpack = (pack_sums, unpack_sums) if first else (pack_int16, unpack_int16)
        with jax.named_scope("scores"):
            if first:
                away, here, kept, low_weights = first_scores(coverage, block_mask, edge_prior, place)
                current = low_weights
            else:
                away = later_scores(False, kept, low_weights, place)
                here = later_scores(True, kept, low_weights, place)
            here = here + lax.ppermute(away, "col", swap(1))
            here = here.reshape(4, -1, here.shape[-1])
        with jax.named_scope("sum_x"):
            parts = [unpack(lax.ppermute(pack(here[d]), "col", ring(16, d, 4))) for d in (1, 2, 3)]
            scores = sum_four([here[0]] + parts)
        if first:
            with jax.named_scope("flip"):
                flipped_here, flipped_away, cost = flip(kept, test_cost, place, scores)
        with jax.named_scope("sum_z"):
            scores = scores + unpack(lax.ppermute(pack(scores), "col", swap(2)))
            ratios = scores[:PAIR] / cost
            low_ratios = ratios.astype(bf16)
            if first:
                sums = [part.astype(bf16) for part in bf16_parts(scores[PAIR:])]
                low_ratios = jnp.concatenate([low_ratios] + sums, axis=0)
        with jax.named_scope("gather"):
            lows = [low_ratios] + [lax.ppermute(low_ratios, "col", ring(16, d, 4)) for d in (1, 2, 3)]
            low_here = jnp.concatenate(lows, axis=0)
            low_away = lax.ppermute(low_here, "col", swap(1))
            if first:
                sums_here, sums_away = low_here, low_away
        with jax.named_scope("total"):
            total = total_load(sums_here, sums_away, low_here, low_away)
            total = float16_parts(pair_sum(total, "depth", 1))
        with jax.named_scope("loads"):
            half, size = loads(half_loads_kernel, flipped_here, low_here)
            load, power = loads(whole_loads_kernel, flipped_away, low_away, half, size)
        with jax.named_scope("sum_y"):
            share = load.shape[0] // 4
            parts = [(load[:share], power, from_parts(*total))]
            for d in (1, 2, 3):
                wire = pack_part(load[d * share : (d + 1) * share], power, total)
                parts.append(unpack_part(lax.ppermute(wire, "row", ring(4, d))))
            part, powers, totals = zip(*parts, strict=True)
            power = jnp.maximum(jnp.maximum(powers[0], powers[1]), jnp.maximum(powers[2], powers[3])) + 2.0
        with jax.named_scope("gather_y"):
            wire = pack_load(sum_four(part), power)
            sent = wire.astype(jnp.float16)
            wires = [wire] + [lax.ppermute(sent, "row", ring(4, -d)).astype(f32) for d in (1, 2, 3)]
        with jax.named_scope("total"):
            total = pair_sum(sum_four(totals), "depth", 2)
        with jax.named_scope("update"):
            if iteration < ITERS - 1:
                current, low_weights = update(wires, total, current, place)
            else:
                current, primal = update(wires, total, current, place, ratios)
    return (current, primal)


def solution(mesh):
    placed = (P("row", "col"), P("row", "col"), P("col", "depth"), P("row", "depth"))
    return jax.shard_map(
        body,
        mesh=mesh,
        in_specs=placed,
        out_specs=(P("col", "depth"), P(("row", "col"), "depth")),
        check_vma=False,
    )
```

time: 124 us -> 121 us (0.976)
  waiting for transfers between devices: 37.8 us -> 41.3 us
  other arithmetic: 5.2 us -> 2.11 us
  local copies, waits for them, and re-layouts: 1.9 us -> 0.3 us
  starting transfers between devices: 55.9 us -> 54.6 us
    ppermute x6, waiting for transfers between devices: 0.02 us -> 7.91 us  [body(): parts.append(unpack_part(lax.ppermute(wire, 'row', ring(4, d))))]
    ppermute x6, waiting for transfers between devices: 5.1 us -> 0.02 us  [body(): lax.ppermute(sent, 'row', ring(4, -d)).astype(f32)]
    unnamed x13 -> x8, local copies, waits for them, and re-layouts: 1.71 us -> 0.17 us
    convert_element_type x3 -> x0, other arithmetic: 1.38 us -> none  [the longest x1 0.95 us: body(): cost = cost.reshape(PAIR, costs.shape[-1]).astype(f32)]
    pallas_call x1, Pallas kernels: 5.97 us -> 4.65 us  [first_scores(): call(first_scores_kernel, [pltpu.VMEM((4 * WITH_SUMS, scen), f32), pltpu....]
  transfers between devices with their start and end apart: 34 -> 34, of which waited for: 21 -> 22; matrix products, arithmetic and copies ran while one was open for 1% -> 0% of each run, Pallas kernels for 7% -> 9%
where the time goes in v2:
time: 121 us; the launch traced here: 120 us
  starting transfers between devices  54.6 us (45%)
  waiting for transfers between devices  41.3 us (34%)
  Pallas kernels  20.3 us (17%)
  other arithmetic  2.11 us (2%)
  between operations  1.42 us (1%)
    ppermute x4, starting transfers between devices, pair_sum(): return value + lax.ppermute(value, axis, [(i, i ^ bit) for i in range(4)])  18.2 us
    ppermute x6, waiting for transfers between devices, body(): lax.ppermute(low_ratios, 'col', ring(16, d, 4))  12.3 us
    ppermute x6, waiting for transfers between devices, body(): lax.ppermute(pack(here[d]), 'col', ring(16, d, 4))  11.2 us
    ppermute x6, starting transfers between devices, body(): lax.ppermute(sent, 'row', ring(4, -d)).astype(f32)  9.71 us
    ppermute x6, starting transfers between devices, body(): lax.ppermute(pack(here[d]), 'col', ring(16, d, 4))  8.82 us
    ppermute x6, waiting for transfers between devices, body(): parts.append(unpack_part(lax.ppermute(wire, 'row', ring(4, d))))  7.91 us
    ppermute x6, starting transfers between devices, body(): parts.append(unpack_part(lax.ppermute(wire, 'row', ring(4, d))))  7.89 us
    ppermute x6, starting transfers between devices, body(): lax.ppermute(low_ratios, 'col', ring(16, d, 4))  6.26 us
  transfers between devices with their start and end apart: 34, of which 22 were waited for; matrix products, arithmetic and copies ran while one was open for 0% of the time, Pallas kernels for 9%

profile of v2, /device:TPU:8, one launch (start us, length us, event | category | flops | bytes accessed | tf_op | source)
XLA Modules:
  0.0 120.0 jit_solution(11556439387156076679)
XLA Ops:
  0.7 4.6 %scores.4 = (f32[1568,128]{1,0:T(8,128)S(1)}, bf16[3072,1024]{1,0:T(8,128)(2,1)S(1)}, bf16[1024,128]{1,0:T(8,128)(2,1)S(1)}) custom-call(s32[4]{0:T(128)S(1)} %pad_add_fusion.place_ref, s32[8,24]{1,0:T(8,128)} %bitcast.29, bf16[3072,1024]{1,0:T(8,128)(2,1)} %cover_ref.1, bf16[1024,128]{1,0:T(8,128)(2,1)} %prior_ref.1), custom_call_target="tpu_custom_call" | custom-call | flops 402653184 | bytes 1006632 | tf_op jit(solution)/shard_map/scores/pallas_call | solution.py:105
  5.5 2.3 %scores.5 = f32[1568,128]{1,0:T(8,128)S(1)} custom-call(s32[4]{0:T(128)S(1)} %pad_add_fusion.place_ref, bf16[3072,1024]{1,0:T(8,128)(2,1)S(1)} %get-tuple-element.18.kept_ref, bf16[1024,128]{1,0:T(8,128)(2,1)S(1)} %get-tuple-element.19.weights_ref.current_ref), custom_call_target="tpu_custom_call" | custom-call | flops 402653184 | bytes 1006632 | tf_op jit(solution)/shard_map/scores/pallas_call | solution.py:121
  8.0 3.1 %collective-permute-start.1 = (bf16[416,128]{1,0:T(8,128)(2,1)S(1)}, bf16[416,128]{1,0:T(8,128)(2,1)S(1)}, u32[]{:S(2)}, u32[]{:S(2)}) collective-permute-start(bf16[416,128]{1,0:T(8,128)(2,1)S(1)} %constant_dynamic-update-slice_fusion), channel_id=1, source_target_pairs={{0,32},{4,36},{8,40},{12,44},{16,48},{20,52},{24,56},{28,60},{32,0... | collective-permute-start | bytes 319496 | tf_op jit(solution)/shard_map/sum_x/ppermute | solution.py:387
  11.2 1.1 collective-permute-start.3
  13.2 4.2 %collective-permute-done.3 = bf16[416,128]{1,0:T(8,128)(2,1)S(1)} collective-permute-done((bf16[416,128]{1,0:T(8,128)(2,1)S(1)}, bf16[416,128]{1,0:T(8,128)(2,1)S(1)}, u32[]{:S(2)}, u32[]{:S(2)}) %collective-permute-start.3) | collective-permute-done | bytes 106528 | tf_op jit(solution)/shard_map/sum_x/ppermute | solution.py:387
  17.4 0.9 collective-permute-done.2
  18.6 2.0 %collective-permute-start.4 = (bf16[416,128]{1,0:T(8,128)(2,1)S(1)}, bf16[416,128]{1,0:T(8,128)(2,1)S(1)}, u32[]{:S(2)}, u32[]{:S(2)}) collective-permute-start(bf16[416,128]{1,0:T(8,128)(2,1)S(1)} %constant_dynamic-update-slice_fusion.15), channel_id=1, source_target_pairs={{0,8},{4,12},{8,0},{12,4},{16,24},{20,28},{24,16},{28,20},{32,40},... | collective-permute-start | bytes 319496 | tf_op jit(solution)/shard_map/sum_z/ppermute | solution.py:393
  20.6 3.0 %flip.1 = (bf16[1024,1536]{1,0:T(8,128)(2,1)S(1)}, bf16[1024,1536]{1,0:T(8,128)(2,1)S(1)}, f32[384,128]{1,0:T(8,128)S(1)}) custom-call(s32[4]{0:T(128)S(1)} %pad_add_fusion.place_ref, bf16[3072,1024]{1,0:T(8,128)(2,1)S(1)} %get-tuple-element.18.kept_ref, s32[3072,128]{1,0:T(8,128)} %cost_ref.1, f32[392,128]{1,0:T(8,128)S(1)} %fusion.4.after_ref), custom_call_target="tpu_custom_call" | custom-call | flops 3221225472 | bytes 8053063 | tf_op jit(solution)/shard_map/flip/pallas_call | solution.py:175
  23.8 2.0 %collective-permute-start.7 = (bf16[416,128]{1,0:T(8,128)(2,1)S(1)}, bf16[416,128]{1,0:T(8,128)(2,1)S(1)}, u32[]{:S(2)}, u32[]{:S(2)}) collective-permute-start(bf16[416,128]{1,0:T(8,128)(2,1)S(1)} %constant_dynamic-update-slice_fusion.20), channel_id=1, source_target_pairs={{0,48},{4,52},{8,56},{12,60},{16,0},{20,4},{24,8},{28,12},{32,16},... | collective-permute-start | bytes 319496 | tf_op jit(solution)/shard_map/gather/ppermute | solution.py:400
  27.5 6.4 %collective-permute-done.5 = bf16[416,128]{1,0:T(8,128)(2,1)S(1)} collective-permute-done((bf16[416,128]{1,0:T(8,128)(2,1)S(1)}, bf16[416,128]{1,0:T(8,128)(2,1)S(1)}, u32[]{:S(2)}, u32[]{:S(2)}) %collective-permute-start.5) | collective-permute-done | bytes 106528 | tf_op jit(solution)/shard_map/gather/ppermute | solution.py:400
  34.2 1.1 loads.4
  36.4 3.4 %collective-permute-start.9 = (f32[8,128]{1,0:T(8,128)S(1)}, f32[8,128]{1,0:T(8,128)S(1)}, u32[]{:S(2)}, u32[]{:S(2)}) collective-permute-start(f32[8,128]{1,0:T(8,128)S(1)} %total.2), channel_id=1, source_target_pairs={{0,1},{1,0},{2,3},{3,2},{4,5},{5,4},{6,7},{7,6},{8,9},{9,8},{10,11... | collective-permute-start | bytes 12296 | tf_op jit(solution)/shard_map/total/ppermute | solution.py:362
  39.8 1.1 loads.5
  41.5 1.7 %collective-permute-start.11 = (f16[288,128]{1,0:T(8,128)(2,1)S(1)}, f16[288,128]{1,0:T(8,128)(2,1)S(1)}, u32[]{:S(2)}, u32[]{:S(2)}) collective-permute-start(f16[288,128]{1,0:T(8,128)(2,1)S(1)} %get-tuple-element.103), channel_id=1, source_target_pairs={{0,64},{64,128},{128,192},{192,0},{1,65},{65,129},{129,193},{193,1... | collective-permute-start | bytes 221192 | tf_op jit(solution)/shard_map/sum_y/ppermute | solution.py:416
  43.6 2.3 %collective-permute-start.10 = (f16[288,128]{1,0:T(8,128)(2,1)S(1)}, f16[288,128]{1,0:T(8,128)(2,1)S(1)}, u32[]{:S(2)}, u32[]{:S(2)}) collective-permute-start(f16[288,128]{1,0:T(8,128)(2,1)S(1)} %get-tuple-element.105), channel_id=1, source_target_pairs={{0,128},{64,192},{128,0},{192,64},{1,129},{65,193},{129,1},{193,65... | collective-permute-start | bytes 221192 | tf_op jit(solution)/shard_map/sum_y/ppermute | solution.py:416
  45.9 2.3 %collective-permute-done.12 = f16[288,128]{1,0:T(8,128)(2,1)S(1)} collective-permute-done((f16[288,128]{1,0:T(8,128)(2,1)S(1)}, f16[288,128]{1,0:T(8,128)(2,1)S(1)}, u32[]{:S(2)}, u32[]{:S(2)}) %collective-permute-start.12) | collective-permute-done | bytes 73760 | tf_op jit(solution)/shard_map/sum_y/ppermute | solution.py:416
  48.2 1.2 collective-permute-done.10
  49.6 1.7 %collective-permute-start.15 = (f16[272,128]{1,0:T(8,128)(2,1)S(1)}, f16[272,128]{1,0:T(8,128)(2,1)S(1)}, u32[]{:S(2)}, u32[]{:S(2)}) collective-permute-start(f16[272,128]{1,0:T(8,128)(2,1)S(1)} %get-tuple-element.90), channel_id=1, source_target_pairs={{0,64},{64,128},{128,192},{192,0},{1,65},{65,129},{129,193},{193,1... | collective-permute-start | bytes 208904 | tf_op jit(solution)/shard_map/gather_y/ppermute | solution.py:422
  51.3 2.1 %collective-permute-start.14 = (f16[272,128]{1,0:T(8,128)(2,1)S(1)}, f16[272,128]{1,0:T(8,128)(2,1)S(1)}, u32[]{:S(2)}, u32[]{:S(2)}) collective-permute-start(f16[272,128]{1,0:T(8,128)(2,1)S(1)} %get-tuple-element.90), channel_id=1, source_target_pairs={{0,128},{64,192},{128,0},{192,64},{1,129},{65,193},{129,1},{193,65... | collective-permute-start | bytes 208904 | tf_op jit(solution)/shard_map/gather_y/ppermute | solution.py:422
  53.5 1.2 collective-permute-start.13
  54.6 6.3 %collective-permute-start.16 = (f32[8,128]{1,0:T(8,128)S(1)}, f32[8,128]{1,0:T(8,128)S(1)}, u32[]{:S(2)}, u32[]{:S(2)}) collective-permute-start(f32[8,128]{1,0:T(8,128)S(1)} %get-tuple-element.71), channel_id=1, source_target_pairs={{0,2},{1,3},{2,0},{3,1},{4,6},{5,7},{6,4},{7,5},{8,10},{9,11},{10,... | collective-permute-start | bytes 12296 | tf_op jit(solution)/shard_map/total/ppermute | solution.py:362
  60.9 1.6 %collective-permute-done.16 = f32[8,128]{1,0:T(8,128)S(1)} collective-permute-done((f32[8,128]{1,0:T(8,128)S(1)}, f32[8,128]{1,0:T(8,128)S(1)}, u32[]{:S(2)}, u32[]{:S(2)}) %collective-permute-start.16) | collective-permute-done | bytes 4128 | tf_op jit(solution)/shard_map/total/ppermute | solution.py:362
  63.2 1.5 %scores.7 = f32[1536,128]{1,0:T(8,128)S(1)} custom-call(s32[4]{0:T(128)S(1)} %pad_add_fusion.place_ref, bf16[3072,1024]{1,0:T(8,128)(2,1)S(1)} %get-tuple-element.18.kept_ref, bf16[1024,128]{1,0:T(8,128)(2,1)S(1)} %get-tuple-element.28.weights_ref), custom_call_target="tpu_custom_call" | custom-call | flops 402653184 | bytes 1006632 | tf_op jit(solution)/shard_map/scores/pallas_call | solution.py:141
  64.9 1.5 %scores.6 = f32[1536,128]{1,0:T(8,128)S(1)} custom-call(s32[4]{0:T(128)S(1)} %pad_add_fusion.place_ref, bf16[3072,1024]{1,0:T(8,128)(2,1)S(1)} %get-tuple-element.18.kept_ref, bf16[1024,128]{1,0:T(8,128)(2,1)S(1)} %get-tuple-element.28.weights_ref), custom_call_target="tpu_custom_call" | custom-call | flops 402653184 | bytes 1006632 | tf_op jit(solution)/shard_map/scores/pallas_call | solution.py:141
  67.6 3.3 %collective-permute-start.20 = (s16[400,128]{1,0:T(8,128)(2,1)S(1)}, s16[400,128]{1,0:T(8,128)(2,1)S(1)}, u32[]{:S(2)}, u32[]{:S(2)}) collective-permute-start(s16[400,128]{1,0:T(8,128)(2,1)S(1)} %fusion.2), channel_id=1, source_target_pairs={{0,48},{4,52},{8,56},{12,60},{16,0},{20,4},{24,8},{28,12},{32,16},... | collective-permute-start | bytes 307208 | tf_op jit(solution)/shard_map/sum_x/ppermute | solution.py:387
  71.2 2.4 %collective-permute-done.19 = s16[400,128]{1,0:T(8,128)(2,1)S(1)} collective-permute-done((s16[400,128]{1,0:T(8,128)(2,1)S(1)}, s16[400,128]{1,0:T(8,128)(2,1)S(1)}, u32[]{:S(2)}, u32[]{:S(2)}) %collective-permute-start.19) | collective-permute-done | bytes 102432 | tf_op jit(solution)/shard_map/sum_x/ppermute | solution.py:387
  73.7 1.5 %collective-permute-done.20 = s16[400,128]{1,0:T(8,128)(2,1)S(1)} collective-permute-done((s16[400,128]{1,0:T(8,128)(2,1)S(1)}, s16[400,128]{1,0:T(8,128)(2,1)S(1)}, u32[]{:S(2)}, u32[]{:S(2)}) %collective-permute-start.20) | collective-permute-done | bytes 102432 | tf_op jit(solution)/shard_map/sum_x/ppermute | solution.py:387
  75.3 2.1 %collective-permute-done.18 = s16[400,128]{1,0:T(8,128)(2,1)S(1)} collective-permute-done((s16[400,128]{1,0:T(8,128)(2,1)S(1)}, s16[400,128]{1,0:T(8,128)(2,1)S(1)}, u32[]{:S(2)}, u32[]{:S(2)}) %collective-permute-start.18) | collective-permute-done | bytes 102432 | tf_op jit(solution)/shard_map/sum_x/ppermute | solution.py:387
  77.6 1.1 collective-permute-start.21
  78.7 3.6 %collective-permute-done.21 = s16[400,128]{1,0:T(8,128)(2,1)S(1)} collective-permute-done((s16[400,128]{1,0:T(8,128)(2,1)S(1)}, s16[400,128]{1,0:T(8,128)(2,1)S(1)}, u32[]{:S(2)}, u32[]{:S(2)}) %collective-permute-start.21) | collective-permute-done | bytes 102432 | tf_op jit(solution)/shard_map/sum_z/ppermute | solution.py:393
  82.5 1.7 %collective-permute-start.24 = (bf16[384,128]{1,0:T(8,128)(2,1)S(1)}, bf16[384,128]{1,0:T(8,128)(2,1)S(1)}, u32[]{:S(2)}, u32[]{:S(2)}) collective-permute-start(bf16[384,128]{1,0:T(8,128)(2,1)S(1)} %get-tuple-element.39), channel_id=1, source_target_pairs={{0,48},{4,52},{8,56},{12,60},{16,0},{20,4},{24,8},{28,12},{32,16},... | collective-permute-start | bytes 294920 | tf_op jit(solution)/shard_map/gather/ppermute | solution.py:400
  84.2 1.0 collective-permute-start.22
  85.2 2.0 %collective-permute-done.24 = bf16[384,128]{1,0:T(8,128)(2,1)S(1)} collective-permute-done((bf16[384,128]{1,0:T(8,128)(2,1)S(1)}, bf16[384,128]{1,0:T(8,128)(2,1)S(1)}, u32[]{:S(2)}, u32[]{:S(2)}) %collective-permute-start.24) | collective-permute-done | bytes 98336 | tf_op jit(solution)/shard_map/gather/ppermute | solution.py:400
  87.2 3.2 %collective-permute-done.23 = bf16[384,128]{1,0:T(8,128)(2,1)S(1)} collective-permute-done((bf16[384,128]{1,0:T(8,128)(2,1)S(1)}, bf16[384,128]{1,0:T(8,128)(2,1)S(1)}, u32[]{:S(2)}, u32[]{:S(2)}) %collective-permute-start.23) | collective-permute-done | bytes 98336 | tf_op jit(solution)/shard_map/gather/ppermute | solution.py:400
  91.2 1.1 loads.6
  93.4 2.7 %collective-permute-start.26 = (f32[8,128]{1,0:T(8,128)S(1)}, f32[8,128]{1,0:T(8,128)S(1)}, u32[]{:S(2)}, u32[]{:S(2)}) collective-permute-start(f32[8,128]{1,0:T(8,128)S(1)} %total.3), channel_id=1, source_target_pairs={{0,1},{1,0},{2,3},{3,2},{4,5},{5,4},{6,7},{7,6},{8,9},{9,8},{10,11... | collective-permute-start | bytes 12296 | tf_op jit(solution)/shard_map/total/ppermute | solution.py:362
  96.0 1.1 loads.7
  98.1 0.9 collective-permute-start.28
  99.0 1.2 collective-permute-start.29
  100.2 1.4 %collective-permute-start.27 = (f16[288,128]{1,0:T(8,128)(2,1)S(1)}, f16[288,128]{1,0:T(8,128)(2,1)S(1)}, u32[]{:S(2)}, u32[]{:S(2)}) collective-permute-start(f16[288,128]{1,0:T(8,128)(2,1)S(1)} %get-tuple-element.94), channel_id=1, source_target_pairs={{0,128},{64,192},{128,0},{192,64},{1,129},{65,193},{129,1},{193,65... | collective-permute-start | bytes 221192 | tf_op jit(solution)/shard_map/sum_y/ppermute | solution.py:416
  101.6 1.2 %collective-permute-done.28 = f16[288,128]{1,0:T(8,128)(2,1)S(1)} collective-permute-done((f16[288,128]{1,0:T(8,128)(2,1)S(1)}, f16[288,128]{1,0:T(8,128)(2,1)S(1)}, u32[]{:S(2)}, u32[]{:S(2)}) %collective-permute-start.28) | collective-permute-done | bytes 73760 | tf_op jit(solution)/shard_map/sum_y/ppermute | solution.py:416
  102.9 1.1 collective-permute-done.29
  104.0 2.0 %collective-permute-done.27 = f16[288,128]{1,0:T(8,128)(2,1)S(1)} collective-permute-done((f16[288,128]{1,0:T(8,128)(2,1)S(1)}, f16[288,128]{1,0:T(8,128)(2,1)S(1)}, u32[]{:S(2)}, u32[]{:S(2)}) %collective-permute-start.27) | collective-permute-done | bytes 73760 | tf_op jit(solution)/shard_map/sum_y/ppermute | solution.py:416
  106.3 0.9 collective-permute-start.32
  107.2 3.8 %collective-permute-start.31 = (f16[272,128]{1,0:T(8,128)(2,1)S(1)}, f16[272,128]{1,0:T(8,128)(2,1)S(1)}, u32[]{:S(2)}, u32[]{:S(2)}) collective-permute-start(f16[272,128]{1,0:T(8,128)(2,1)S(1)} %get-tuple-element.88), channel_id=1, source_target_pairs={{0,128},{64,192},{128,0},{192,64},{1,129},{65,193},{129,1},{193,65... | collective-permute-start | bytes 208904 | tf_op jit(solution)/shard_map/gather_y/ppermute | solution.py:422
  111.0 5.9 %collective-permute-start.33 = (f32[8,128]{1,0:T(8,128)S(1)}, f32[8,128]{1,0:T(8,128)S(1)}, u32[]{:S(2)}, u32[]{:S(2)}) collective-permute-start(f32[8,128]{1,0:T(8,128)S(1)} %get-tuple-element.69), channel_id=1, source_target_pairs={{0,2},{1,3},{2,0},{3,1},{4,6},{5,7},{6,4},{7,5},{8,10},{9,11},{10,... | collective-permute-start | bytes 12296 | tf_op jit(solution)/shard_map/total/ppermute | solution.py:362
  116.9 1.6 %collective-permute-done.33 = f32[8,128]{1,0:T(8,128)S(1)} collective-permute-done((f32[8,128]{1,0:T(8,128)S(1)}, f32[8,128]{1,0:T(8,128)S(1)}, u32[]{:S(2)}, u32[]{:S(2)}) %collective-permute-start.33) | collective-permute-done | bytes 4128 | tf_op jit(solution)/shard_map/total/ppermute | solution.py:362
  118.6 1.4 %update.3 = (f32[1024,128]{1,0:T(8,128)}, f32[192,128]{1,0:T(8,128)}) custom-call(s32[4]{0:T(128)S(1)} %pad_add_fusion.place_ref, f32[272,128]{1,0:T(8,128)S(1)} %get-tuple-element.89.zero, f32[272,128]{1,0:T(8,128)S(1)} %convert_element_type.164.one, f32[272,128]{1,0:T(8,128)S(1)} %convert_element_type.165.two, f32[272,128]{1,0:T(8,128)S(1)} %convert_element_type.166.three, ...), custom_call_target="tpu_custom_call" | custom-call | flops 10000000 | bytes 25000 | tf_op jit(solution)/shard_map/update/pallas_call | solution.py:344
  (139 shorter events, 11.7 us)
Async XLA Ops:
  5.4 2.4 %collective-permute-start = (f32[1568,128]{1,0:T(8,128)S(1)}, f32[1568,128]{1,0:T(8,128)S(1)}, u32[]{:S(2)}, u32[]{:S(2)}) collective-permute-start(f32[1568,128]{1,0:T(8,128)S(1)} %get-tuple-element.20), channel_id=1, source_target_pairs={{0,4},{4,0},{8,12},{12,8},{16,20},{20,16},{24,28},{28,24},{32,36},... | collective-permute-start | bytes 2408456 | tf_op jit(solution)/shard_map/scores/ppermute | solution.py:384
  8.0 10.3 %collective-permute-start.1 = (bf16[416,128]{1,0:T(8,128)(2,1)S(1)}, bf16[416,128]{1,0:T(8,128)(2,1)S(1)}, u32[]{:S(2)}, u32[]{:S(2)}) collective-permute-start(bf16[416,128]{1,0:T(8,128)(2,1)S(1)} %constant_dynamic-update-slice_fusion), channel_id=1, source_target_pairs={{0,32},{4,36},{8,40},{12,44},{16,48},{20,52},{24,56},{28,60},{32,0... | collective-permute-start | bytes 319496 | tf_op jit(solution)/shard_map/sum_x/ppermute | solution.py:387
  11.2 6.2 %collective-permute-start.3 = (bf16[416,128]{1,0:T(8,128)(2,1)S(1)}, bf16[416,128]{1,0:T(8,128)(2,1)S(1)}, u32[]{:S(2)}, u32[]{:S(2)}) collective-permute-start(bf16[416,128]{1,0:T(8,128)(2,1)S(1)} %constant_dynamic-update-slice_fusion.10), channel_id=1, source_target_pairs={{0,48},{4,52},{8,56},{12,60},{16,0},{20,4},{24,8},{28,12},{32,16},... | collective-permute-start | bytes 319496 | tf_op jit(solution)/shard_map/sum_x/ppermute | solution.py:387
  12.3 6.0 %collective-permute-start.2 = (bf16[416,128]{1,0:T(8,128)(2,1)S(1)}, bf16[416,128]{1,0:T(8,128)(2,1)S(1)}, u32[]{:S(2)}, u32[]{:S(2)}) collective-permute-start(bf16[416,128]{1,0:T(8,128)(2,1)S(1)} %constant_dynamic-update-slice_fusion.5), channel_id=1, source_target_pairs={{0,16},{4,20},{8,24},{12,28},{16,32},{20,36},{24,40},{28,44},{32,4... | collective-permute-start | bytes 319496 | tf_op jit(solution)/shard_map/sum_x/ppermute | solution.py:387
  18.6 5.0 %collective-permute-start.4 = (bf16[416,128]{1,0:T(8,128)(2,1)S(1)}, bf16[416,128]{1,0:T(8,128)(2,1)S(1)}, u32[]{:S(2)}, u32[]{:S(2)}) collective-permute-start(bf16[416,128]{1,0:T(8,128)(2,1)S(1)} %constant_dynamic-update-slice_fusion.15), channel_id=1, source_target_pairs={{0,8},{4,12},{8,0},{12,4},{16,24},{20,28},{24,16},{28,20},{32,40},... | collective-permute-start | bytes 319496 | tf_op jit(solution)/shard_map/sum_z/ppermute | solution.py:393
  23.8 10.0 %collective-permute-start.7 = (bf16[416,128]{1,0:T(8,128)(2,1)S(1)}, bf16[416,128]{1,0:T(8,128)(2,1)S(1)}, u32[]{:S(2)}, u32[]{:S(2)}) collective-permute-start(bf16[416,128]{1,0:T(8,128)(2,1)S(1)} %constant_dynamic-update-slice_fusion.20), channel_id=1, source_target_pairs={{0,48},{4,52},{8,56},{12,60},{16,0},{20,4},{24,8},{28,12},{32,16},... | collective-permute-start | bytes 319496 | tf_op jit(solution)/shard_map/gather/ppermute | solution.py:400
  25.8 8.0 %collective-permute-start.6 = (bf16[416,128]{1,0:T(8,128)(2,1)S(1)}, bf16[416,128]{1,0:T(8,128)(2,1)S(1)}, u32[]{:S(2)}, u32[]{:S(2)}) collective-permute-start(bf16[416,128]{1,0:T(8,128)(2,1)S(1)} %constant_dynamic-update-slice_fusion.20), channel_id=1, source_target_pairs={{0,32},{4,36},{8,40},{12,44},{16,48},{20,52},{24,56},{28,60},{32,0... | collective-permute-start | bytes 319496 | tf_op jit(solution)/shard_map/gather/ppermute | solution.py:400
  26.6 7.2 %collective-permute-start.5 = (bf16[416,128]{1,0:T(8,128)(2,1)S(1)}, bf16[416,128]{1,0:T(8,128)(2,1)S(1)}, u32[]{:S(2)}, u32[]{:S(2)}) collective-permute-start(bf16[416,128]{1,0:T(8,128)(2,1)S(1)} %constant_dynamic-update-slice_fusion.20), channel_id=1, source_target_pairs={{0,16},{4,20},{8,24},{12,28},{16,32},{20,36},{24,40},{28,44},{32,4... | collective-permute-start | bytes 319496 | tf_op jit(solution)/shard_map/gather/ppermute | solution.py:400
  33.9 2.0 %collective-permute-start.8 = (bf16[1664,128]{1,0:T(8,128)(2,1)S(1)}, bf16[1664,128]{1,0:T(8,128)(2,1)S(1)}, u32[]{:S(2)}, u32[]{:S(2)}) collective-permute-start(bf16[1664,128]{1,0:T(8,128)(2,1)S(1)} %constant_dynamic-update-slice_fusion.25.low_ref.sums_own.low_own), channel_id=1, source_target_pairs={{0,4},{4,0},{8,12},{12,8},{16,20},{20,16},{24,28},{28,24},{32,36},... | collective-permute-start | bytes 1277960 | tf_op jit(solution)/shard_map/gather/ppermute | solution.py:402
  36.4 4.9 %collective-permute-start.9 = (f32[8,128]{1,0:T(8,128)S(1)}, f32[8,128]{1,0:T(8,128)S(1)}, u32[]{:S(2)}, u32[]{:S(2)}) collective-permute-start(f32[8,128]{1,0:T(8,128)S(1)} %total.2), channel_id=1, source_target_pairs={{0,1},{1,0},{2,3},{3,2},{4,5},{5,4},{6,7},{7,6},{8,9},{9,8},{10,11... | collective-permute-start | bytes 12296 | tf_op jit(solution)/shard_map/total/ppermute | solution.py:362
  41.5 4.4 %collective-permute-start.11 = (f16[288,128]{1,0:T(8,128)(2,1)S(1)}, f16[288,128]{1,0:T(8,128)(2,1)S(1)}, u32[]{:S(2)}, u32[]{:S(2)}) collective-permute-start(f16[288,128]{1,0:T(8,128)(2,1)S(1)} %get-tuple-element.103), channel_id=1, source_target_pairs={{0,64},{64,128},{128,192},{192,0},{1,65},{65,129},{129,193},{193,1... | collective-permute-start | bytes 221192 | tf_op jit(solution)/shard_map/sum_y/ppermute | solution.py:416
  43.1 5.1 %collective-permute-start.12 = (f16[288,128]{1,0:T(8,128)(2,1)S(1)}, f16[288,128]{1,0:T(8,128)(2,1)S(1)}, u32[]{:S(2)}, u32[]{:S(2)}) collective-permute-start(f16[288,128]{1,0:T(8,128)(2,1)S(1)} %get-tuple-element.104), channel_id=1, source_target_pairs={{0,192},{64,0},{128,64},{192,128},{1,193},{65,1},{129,65},{193,129... | collective-permute-start | bytes 221192 | tf_op jit(solution)/shard_map/sum_y/ppermute | solution.py:416
  43.6 5.9 %collective-permute-start.10 = (f16[288,128]{1,0:T(8,128)(2,1)S(1)}, f16[288,128]{1,0:T(8,128)(2,1)S(1)}, u32[]{:S(2)}, u32[]{:S(2)}) collective-permute-start(f16[288,128]{1,0:T(8,128)(2,1)S(1)} %get-tuple-element.105), channel_id=1, source_target_pairs={{0,128},{64,192},{128,0},{192,64},{1,129},{65,193},{129,1},{193,65... | collective-permute-start | bytes 221192 | tf_op jit(solution)/shard_map/sum_y/ppermute | solution.py:416
  49.6 12.9 %collective-permute-start.15 = (f16[272,128]{1,0:T(8,128)(2,1)S(1)}, f16[272,128]{1,0:T(8,128)(2,1)S(1)}, u32[]{:S(2)}, u32[]{:S(2)}) collective-permute-start(f16[272,128]{1,0:T(8,128)(2,1)S(1)} %get-tuple-element.90), channel_id=1, source_target_pairs={{0,64},{64,128},{128,192},{192,0},{1,65},{65,129},{129,193},{193,1... | collective-permute-start | bytes 208904 | tf_op jit(solution)/shard_map/gather_y/ppermute | solution.py:422
  51.3 11.2 %collective-permute-start.14 = (f16[272,128]{1,0:T(8,128)(2,1)S(1)}, f16[272,128]{1,0:T(8,128)(2,1)S(1)}, u32[]{:S(2)}, u32[]{:S(2)}) collective-permute-start(f16[272,128]{1,0:T(8,128)(2,1)S(1)} %get-tuple-element.90), channel_id=1, source_target_pairs={{0,128},{64,192},{128,0},{192,64},{1,129},{65,193},{129,1},{193,65... | collective-permute-start | bytes 208904 | tf_op jit(solution)/shard_map/gather_y/ppermute | solution.py:422
  53.5 9.1 %collective-permute-start.13 = (f16[272,128]{1,0:T(8,128)(2,1)S(1)}, f16[272,128]{1,0:T(8,128)(2,1)S(1)}, u32[]{:S(2)}, u32[]{:S(2)}) collective-permute-start(f16[272,128]{1,0:T(8,128)(2,1)S(1)} %get-tuple-element.90), channel_id=1, source_target_pairs={{0,192},{64,0},{128,64},{192,128},{1,193},{65,1},{129,65},{193,129... | collective-permute-start | bytes 208904 | tf_op jit(solution)/shard_map/gather_y/ppermute | solution.py:422
  54.6 7.8 %collective-permute-start.16 = (f32[8,128]{1,0:T(8,128)S(1)}, f32[8,128]{1,0:T(8,128)S(1)}, u32[]{:S(2)}, u32[]{:S(2)}) collective-permute-start(f32[8,128]{1,0:T(8,128)S(1)} %get-tuple-element.71), channel_id=1, source_target_pairs={{0,2},{1,3},{2,0},{3,1},{4,6},{5,7},{6,4},{7,5},{8,10},{9,11},{10,... | collective-permute-start | bytes 12296 | tf_op jit(solution)/shard_map/total/ppermute | solution.py:362
  64.8 2.4 %collective-permute-start.17 = (f32[1536,128]{1,0:T(8,128)S(1)}, f32[1536,128]{1,0:T(8,128)S(1)}, u32[]{:S(2)}, u32[]{:S(2)}) collective-permute-start(f32[1536,128]{1,0:T(8,128)S(1)} %scores.7), channel_id=1, source_target_pairs={{0,4},{4,0},{8,12},{12,8},{16,20},{20,16},{24,28},{28,24},{32,36},... | collective-permute-start | bytes 2359304 | tf_op jit(solution)/shard_map/scores/ppermute | solution.py:384
  67.5 6.2 %collective-permute-start.19 = (s16[400,128]{1,0:T(8,128)(2,1)S(1)}, s16[400,128]{1,0:T(8,128)(2,1)S(1)}, u32[]{:S(2)}, u32[]{:S(2)}) collective-permute-start(s16[400,128]{1,0:T(8,128)(2,1)S(1)} %fusion.1), channel_id=1, source_target_pairs={{0,16},{4,20},{8,24},{12,28},{16,32},{20,36},{24,40},{28,44},{32,4... | collective-permute-start | bytes 307208 | tf_op jit(solution)/shard_map/sum_x/ppermute | solution.py:387
  67.6 7.6 %collective-permute-start.20 = (s16[400,128]{1,0:T(8,128)(2,1)S(1)}, s16[400,128]{1,0:T(8,128)(2,1)S(1)}, u32[]{:S(2)}, u32[]{:S(2)}) collective-permute-start(s16[400,128]{1,0:T(8,128)(2,1)S(1)} %fusion.2), channel_id=1, source_target_pairs={{0,48},{4,52},{8,56},{12,60},{16,0},{20,4},{24,8},{28,12},{32,16},... | collective-permute-start | bytes 307208 | tf_op jit(solution)/shard_map/sum_x/ppermute | solution.py:387
  70.9 6.5 %collective-permute-start.18 = (s16[400,128]{1,0:T(8,128)(2,1)S(1)}, s16[400,128]{1,0:T(8,128)(2,1)S(1)}, u32[]{:S(2)}, u32[]{:S(2)}) collective-permute-start(s16[400,128]{1,0:T(8,128)(2,1)S(1)} %fusion), channel_id=1, source_target_pairs={{0,32},{4,36},{8,40},{12,44},{16,48},{20,52},{24,56},{28,60},{32,0... | collective-permute-start | bytes 307208 | tf_op jit(solution)/shard_map/sum_x/ppermute | solution.py:387
  77.6 4.7 %collective-permute-start.21 = (s16[400,128]{1,0:T(8,128)(2,1)S(1)}, s16[400,128]{1,0:T(8,128)(2,1)S(1)}, u32[]{:S(2)}, u32[]{:S(2)}) collective-permute-start(s16[400,128]{1,0:T(8,128)(2,1)S(1)} %fusion.3), channel_id=1, source_target_pairs={{0,8},{4,12},{8,0},{12,4},{16,24},{20,28},{24,16},{28,20},{32,40},... | collective-permute-start | bytes 307208 | tf_op jit(solution)/shard_map/sum_z/ppermute | solution.py:393
  82.5 4.7 %collective-permute-start.24 = (bf16[384,128]{1,0:T(8,128)(2,1)S(1)}, bf16[384,128]{1,0:T(8,128)(2,1)S(1)}, u32[]{:S(2)}, u32[]{:S(2)}) collective-permute-start(bf16[384,128]{1,0:T(8,128)(2,1)S(1)} %get-tuple-element.39), channel_id=1, source_target_pairs={{0,48},{4,52},{8,56},{12,60},{16,0},{20,4},{24,8},{28,12},{32,16},... | collective-permute-start | bytes 294920 | tf_op jit(solution)/shard_map/gather/ppermute | solution.py:400
  84.2 6.2 %collective-permute-start.23 = (bf16[384,128]{1,0:T(8,128)(2,1)S(1)}, bf16[384,128]{1,0:T(8,128)(2,1)S(1)}, u32[]{:S(2)}, u32[]{:S(2)}) collective-permute-start(bf16[384,128]{1,0:T(8,128)(2,1)S(1)} %get-tuple-element.39), channel_id=1, source_target_pairs={{0,32},{4,36},{8,40},{12,44},{16,48},{20,52},{24,56},{28,60},{32,0... | collective-permute-start | bytes 294920 | tf_op jit(solution)/shard_map/gather/ppermute | solution.py:400
  84.2 6.9 %collective-permute-start.22 = (bf16[384,128]{1,0:T(8,128)(2,1)S(1)}, bf16[384,128]{1,0:T(8,128)(2,1)S(1)}, u32[]{:S(2)}, u32[]{:S(2)}) collective-permute-start(bf16[384,128]{1,0:T(8,128)(2,1)S(1)} %get-tuple-element.39), channel_id=1, source_target_pairs={{0,16},{4,20},{8,24},{12,28},{16,32},{20,36},{24,40},{28,44},{32,4... | collective-permute-start | bytes 294920 | tf_op jit(solution)/shard_map/gather/ppermute | solution.py:400
  91.1 1.8 %collective-permute-start.25 = (bf16[1536,128]{1,0:T(8,128)(2,1)S(1)}, bf16[1536,128]{1,0:T(8,128)(2,1)S(1)}, u32[]{:S(2)}, u32[]{:S(2)}) collective-permute-start(bf16[1536,128]{1,0:T(8,128)(2,1)S(1)} %pad_maximum_fusion.low_ref.low_own), channel_id=1, source_target_pairs={{0,4},{4,0},{8,12},{12,8},{16,20},{20,16},{24,28},{28,24},{32,36},... | collective-permute-start | bytes 1179656 | tf_op jit(solution)/shard_map/gather/ppermute | solution.py:402
  93.4 4.6 %collective-permute-start.26 = (f32[8,128]{1,0:T(8,128)S(1)}, f32[8,128]{1,0:T(8,128)S(1)}, u32[]{:S(2)}, u32[]{:S(2)}) collective-permute-start(f32[8,128]{1,0:T(8,128)S(1)} %total.3), channel_id=1, source_target_pairs={{0,1},{1,0},{2,3},{3,2},{4,5},{5,4},{6,7},{7,6},{8,9},{9,8},{10,11... | collective-permute-start | bytes 12296 | tf_op jit(solution)/shard_map/total/ppermute | solution.py:362
  98.1 4.7 %collective-permute-start.28 = (f16[288,128]{1,0:T(8,128)(2,1)S(1)}, f16[288,128]{1,0:T(8,128)(2,1)S(1)}, u32[]{:S(2)}, u32[]{:S(2)}) collective-permute-start(f16[288,128]{1,0:T(8,128)(2,1)S(1)} %get-tuple-element.92), channel_id=1, source_target_pairs={{0,64},{64,128},{128,192},{192,0},{1,65},{65,129},{129,193},{193,1... | collective-permute-start | bytes 221192 | tf_op jit(solution)/shard_map/sum_y/ppermute | solution.py:416
  99.0 5.0 %collective-permute-start.29 = (f16[288,128]{1,0:T(8,128)(2,1)S(1)}, f16[288,128]{1,0:T(8,128)(2,1)S(1)}, u32[]{:S(2)}, u32[]{:S(2)}) collective-permute-start(f16[288,128]{1,0:T(8,128)(2,1)S(1)} %get-tuple-element.93), channel_id=1, source_target_pairs={{0,192},{64,0},{128,64},{192,128},{1,193},{65,1},{129,65},{193,129... | collective-permute-start | bytes 221192 | tf_op jit(solution)/shard_map/sum_y/ppermute | solution.py:416
  100.2 5.9 %collective-permute-start.27 = (f16[288,128]{1,0:T(8,128)(2,1)S(1)}, f16[288,128]{1,0:T(8,128)(2,1)S(1)}, u32[]{:S(2)}, u32[]{:S(2)}) collective-permute-start(f16[288,128]{1,0:T(8,128)(2,1)S(1)} %get-tuple-element.94), channel_id=1, source_target_pairs={{0,128},{64,192},{128,0},{192,64},{1,129},{65,193},{129,1},{193,65... | collective-permute-start | bytes 221192 | tf_op jit(solution)/shard_map/sum_y/ppermute | solution.py:416
  106.3 12.2 %collective-permute-start.32 = (f16[272,128]{1,0:T(8,128)(2,1)S(1)}, f16[272,128]{1,0:T(8,128)(2,1)S(1)}, u32[]{:S(2)}, u32[]{:S(2)}) collective-permute-start(f16[272,128]{1,0:T(8,128)(2,1)S(1)} %get-tuple-element.88), channel_id=1, source_target_pairs={{0,64},{64,128},{128,192},{192,0},{1,65},{65,129},{129,193},{193,1... | collective-permute-start | bytes 208904 | tf_op jit(solution)/shard_map/gather_y/ppermute | solution.py:422
  107.2 11.3 %collective-permute-start.31 = (f16[272,128]{1,0:T(8,128)(2,1)S(1)}, f16[272,128]{1,0:T(8,128)(2,1)S(1)}, u32[]{:S(2)}, u32[]{:S(2)}) collective-permute-start(f16[272,128]{1,0:T(8,128)(2,1)S(1)} %get-tuple-element.88), channel_id=1, source_target_pairs={{0,128},{64,192},{128,0},{192,64},{1,129},{65,193},{129,1},{193,65... | collective-permute-start | bytes 208904 | tf_op jit(solution)/shard_map/gather_y/ppermute | solution.py:422
  111.0 7.6 %collective-permute-start.30 = (f16[272,128]{1,0:T(8,128)(2,1)S(1)}, f16[272,128]{1,0:T(8,128)(2,1)S(1)}, u32[]{:S(2)}, u32[]{:S(2)}) collective-permute-start(f16[272,128]{1,0:T(8,128)(2,1)S(1)} %get-tuple-element.88), channel_id=1, source_target_pairs={{0,192},{64,0},{128,64},{192,128},{1,193},{65,1},{129,65},{193,129... | collective-permute-start | bytes 208904 | tf_op jit(solution)/shard_map/gather_y/ppermute | solution.py:422
  111.0 7.5 %collective-permute-start.33 = (f32[8,128]{1,0:T(8,128)S(1)}, f32[8,128]{1,0:T(8,128)S(1)}, u32[]{:S(2)}, u32[]{:S(2)}) collective-permute-start(f32[8,128]{1,0:T(8,128)S(1)} %get-tuple-element.69), channel_id=1, source_target_pairs={{0,2},{1,3},{2,0},{3,1},{4,6},{5,7},{6,4},{7,5},{8,10},{9,11},{10,... | collective-permute-start | bytes 12296 | tf_op jit(solution)/shard_map/total/ppermute | solution.py:362
